TPU v7x, 512 devices: a whole 4x4x16 slice. The times are simulated.
512 devices in a mesh: dp: 32 (over z, y_lo), tensor: 16 (over x, y_hi, core).
Axes of the slice: x: 4, y: 4 (y_hi: 2, y_lo: 2; y = y_hi * 2 + y_lo), z: 16, core: 2. Of those that a mesh axis runs over, the one named last changes fastest.
Arguments:
- q_states: bfloat16 [65536, 4096], P(('dp', 'tensor')), may hold values from -500 to 500
- k_states: bfloat16 [65536, 512], P(('dp', 'tensor')), may hold values from -650 to 650
- v_states: bfloat16 [65536, 512], P(('dp', 'tensor')), may hold values from -6 to 6
- q_gain: float32 [128], replicated, may hold values from 0.3 to 7
- k_gain: float32 [128], replicated, may hold values from 0.3 to 7
- out_grad: bfloat16 [65536, 4096], P(('dp', 'tensor')), may hold values from -6 to 6
- lengths: int32 [32, 4], P('dp'), may hold values from 1 to 1024, 2048 in all within a row
- advantage: int32 [65536], P(('dp', 'tensor')), may hold values from -64 to 64
Outputs:
- q_grad: bfloat16 [65536, 4096], P(('dp', 'tensor'))
- k_grad: bfloat16 [65536, 512], P(('dp', 'tensor'))
- v_grad: bfloat16 [65536, 512], P(('dp', 'tensor'))
- gain_grad: float32 [2, 128], replicated
All inputs are finite; a program needn't handle non-finite values.
Results may differ from a plain program's by a relative error of at most 0.02.
The roundings to bfloat16 on the way count: a program that leaves them out, or rounds other values in their place, can miss the bound.
Values may be sent and summed in bfloat16 or wider, within the bound.
No kernel may reach another device: no remote copies, remote signals or barrier semaphores. Data moves between devices by JAX's collectives and lax.ppermute only.
A program may use at most 128 MiB of HBM per device.

v0:
```python
import math

import jax
import jax.numpy as jnp
from jax import lax
from jax.sharding import PartitionSpec as P

HD = 128


rope_base = 1000000.0
norm_eps = 1e-06


def response_layout(lens, group_rows):
    end_marks = jnp.cumsum(lens)
    token_place = jnp.arange(group_rows, dtype=jnp.int32)
    has_ended = end_marks[None, :] <= token_place[:, None]
    resp_start = jnp.sum(jnp.where(has_ended, lens[None, :], 0), axis=1)
    segment = jnp.sum(has_ended.astype(jnp.int32), axis=1)
    owner_mask = segment[:, None] == jnp.arange(lens.shape[0], dtype=jnp.int32)[None, :]
    length = jnp.sum(jnp.where(owner_mask, lens[None, :], 0), axis=1)
    return (token_place - resp_start, segment, length)


def rope_tables(position, head_width):
    half_width = head_width // 2
    frequency = rope_base ** (-jnp.arange(half_width, dtype=jnp.float32) * 2.0 / head_width)
    angles = position.astype(jnp.float32)[:, None] * frequency[None, :]
    cosine = jnp.concatenate([jnp.cos(angles), jnp.cos(angles)], axis=1)
    sine_table = jnp.concatenate([jnp.sin(angles), jnp.sin(angles)], axis=1)
    return (cosine[:, None, :], sine_table[:, None, :])


def half_turn(values):
    half_width = values.shape[-1] // 2
    return jnp.concatenate([-values[..., half_width:], values[..., :half_width]], axis=-1)


def turn_back(values):
    half_width = values.shape[-1] // 2
    return jnp.concatenate([values[..., half_width:], -values[..., :half_width]], axis=-1)


def norm_rope(states, gain_vec, cosine, sine_table):
    values = states.astype(jnp.float32)
    rms_scale = jnp.sqrt(jnp.mean(values * values, axis=-1, keepdims=True) + norm_eps)
    unit_rows = values / rms_scale
    scaled = unit_rows * gain_vec
    turned = scaled * cosine + half_turn(scaled) * sine_table
    return (turned.astype(jnp.bfloat16), unit_rows, rms_scale)


def norm_rope_back(upstream, unit_rows, rms_scale, gain_vec, cosine, sine_table):
    d_scaled = upstream * cosine + turn_back(upstream * sine_table)
    gain_part = jnp.sum(d_scaled * unit_rows, axis=(0, 1))
    d_unit = d_scaled * gain_vec
    d_states = (
        d_unit - unit_rows * jnp.mean(d_unit * unit_rows, axis=-1, keepdims=True)
    ) / rms_scale
    return (d_states.astype(jnp.bfloat16), gain_part)


def local(q_states, k_states, v_states, q_gain, k_gain, out_grad, lengths, advantage):
    tensor_size = lax.axis_size("tensor")
    tensor_pos = lax.axis_index("tensor")
    tok_rows = q_states.shape[0]
    group_rows = tok_rows * tensor_size
    all_heads = q_states.shape[1] // HD
    kv_heads = k_states.shape[1] // HD
    local_heads = all_heads // tensor_size
    copies = tensor_size // kv_heads
    longest = group_rows // 2
    block_rows = min(256, group_rows)
    window = min(block_rows + longest, group_rows)
    resp_count = lengths.shape[1]
    position, segment, length = response_layout(lengths[0], group_rows)
    own_first = tensor_pos * tok_rows
    own_pos = lax.dynamic_slice_in_dim(position, own_first, tok_rows, 0)
    own_len = lax.dynamic_slice_in_dim(length, own_first, tok_rows, 0)
    cos_own, sin_own = rope_tables(own_pos, HD)
    weight = (
        advantage.astype(jnp.float32)
        / 32.0
        * (group_rows / resp_count)
        / own_len.astype(jnp.float32)
    )
    d_out = (
        out_grad.astype(jnp.float32).reshape(tok_rows, all_heads, HD) * weight[:, None, None]
    ).astype(jnp.bfloat16)
    d_out_split = d_out.reshape(tok_rows, tensor_size, local_heads * HD)
    k_turned, k_unit, k_scale = norm_rope(
        k_states.reshape(tok_rows, kv_heads, HD), k_gain, cos_own, sin_own
    )
    q_turned, q_unit, q_scale = norm_rope(
        q_states.reshape(tok_rows, all_heads, HD), q_gain, cos_own, sin_own
    )
    q_arrived, d_arrived = (
        lax.all_to_all(
            q_turned.reshape(tok_rows, tensor_size, local_heads * HD),
            "tensor",
            split_axis=1,
            concat_axis=0,
            tiled=True,
        ),
        lax.all_to_all(d_out_split, "tensor", split_axis=1, concat_axis=0, tiled=True),
    )
    q_heads = q_arrived.reshape(group_rows, local_heads, HD)
    d_heads = d_arrived.reshape(group_rows, local_heads, HD)
    k_all, v_all = (
        lax.all_gather(k_turned.reshape(tok_rows, kv_heads * HD), "tensor", axis=0, tiled=True),
        lax.all_gather(v_states, "tensor", axis=0, tiled=True),
    )
    kv_group = tensor_pos // copies
    key_rows = lax.dynamic_slice_in_dim(k_all, kv_group * HD, HD, 1)
    value_rows = lax.dynamic_slice_in_dim(v_all, kv_group * HD, HD, 1)
    score_scale = 1.0 / math.sqrt(HD)

    def attend(step_index, state_pair):
        d_kv, d_query = state_pair
        q_first = (step_index * block_rows).astype(jnp.int32)
        k_first = jnp.clip(q_first - longest, 0, group_rows - window)
        q_block = lax.dynamic_slice_in_dim(q_heads, q_first, block_rows, 0)
        g_block = lax.dynamic_slice_in_dim(d_heads, q_first, block_rows, 0)
        k_block = lax.dynamic_slice_in_dim(key_rows, k_first, window, 0)
        v_block = lax.dynamic_slice_in_dim(value_rows, k_first, window, 0)
        q_place = q_first + jnp.arange(block_rows, dtype=jnp.int32)
        k_place = k_first + jnp.arange(window, dtype=jnp.int32)
        q_seg = lax.dynamic_slice_in_dim(segment, q_first, block_rows, 0)
        k_seg = lax.dynamic_slice_in_dim(segment, k_first, window, 0)
        allowed = (k_place[None, :] <= q_place[:, None]) & (k_seg[None, :] == q_seg[:, None])
        scores = (
            jnp.einsum("ihd,jd->hij", q_block, k_block, preferred_element_type=jnp.float32)
            * score_scale
        )
        scores = jnp.where(allowed, scores, -1e30)
        peak = jnp.max(scores, axis=-1, keepdims=True)
        expo_rows = jnp.exp(scores - peak)
        prob_block = expo_rows / jnp.sum(expo_rows, axis=-1, keepdims=True)
        prob_round = prob_block.astype(jnp.bfloat16)
        dv_part = jnp.einsum("hij,ihd->jd", prob_round, g_block, preferred_element_type=jnp.float32)
        d_prob = jnp.einsum("ihd,jd->hij", g_block, v_block, preferred_element_type=jnp.float32)
        row_delta = jnp.sum(prob_block * d_prob, axis=-1, keepdims=True)
        d_score = (prob_block * (d_prob - row_delta) * score_scale).astype(jnp.bfloat16)
        dq_block = jnp.einsum("hij,jd->ihd", d_score, k_block, preferred_element_type=jnp.float32)
        dk_part = jnp.einsum("hij,ihd->jd", d_score, q_block, preferred_element_type=jnp.float32)
        kv_part = jnp.concatenate([dk_part, dv_part], axis=1)
        d_kv = lax.dynamic_update_slice_in_dim(
            d_kv, lax.dynamic_slice_in_dim(d_kv, k_first, window, 0) + kv_part, k_first, 0
        )
        d_query = lax.dynamic_update_slice_in_dim(d_query, dq_block, q_first, 0)
        return (d_kv, d_query)

    start_pair = (
        jnp.zeros((group_rows, 2 * HD), jnp.float32),
        jnp.zeros((group_rows, local_heads, HD), jnp.float32),
    )
    d_kv, d_query = lax.fori_loop(0, group_rows // block_rows, attend, start_pair)
    d_kv = d_kv.reshape(group_rows, 1, 2 * HD)
    dq_tokens, dkv_tokens = (
        lax.all_to_all(d_query, "tensor", split_axis=0, concat_axis=1, tiled=True),
        lax.all_to_all(d_kv, "tensor", split_axis=0, concat_axis=1, tiled=True),
    )
    q_grad, q_part = norm_rope_back(dq_tokens, q_unit, q_scale, q_gain, cos_own, sin_own)
    dkv_summed = jnp.sum(dkv_tokens.reshape(tok_rows, kv_heads, copies, 2 * HD), axis=2)
    k_grad, k_part = norm_rope_back(
        dkv_summed[:, :, :HD], k_unit, k_scale, k_gain, cos_own, sin_own
    )
    v_grad = dkv_summed[:, :, HD:].astype(jnp.bfloat16)
    summed = lax.psum((q_part, k_part), ("dp", "tensor"))
    gain_grad = jnp.stack([summed[0], summed[1]]) / group_rows
    return (
        q_grad.reshape(tok_rows, all_heads * HD),
        k_grad.reshape(tok_rows, kv_heads * HD),
        v_grad.reshape(tok_rows, kv_heads * HD),
        gain_grad,
    )


def solution(mesh):
    return jax.shard_map(
        local,
        mesh=mesh,
        in_specs=(
            P(("dp", "tensor"), None),
            P(("dp", "tensor"), None),
            P(("dp", "tensor"), None),
            P(),
            P(),
            P(("dp", "tensor"), None),
            P("dp", None),
            P(("dp", "tensor")),
        ),
        out_specs=(
            P(("dp", "tensor"), None),
            P(("dp", "tensor"), None),
            P(("dp", "tensor"), None),
            P(),
        ),
        check_vma=False,
    )
```

profile of v0, /device:TPU:1, one launch (start us, length us, event | category | flops | bytes accessed | tf_op | source)
XLA Modules:
  0.0 637.7 jit_solution(9292665951579891367)
XLA Ops:
  18.5 10.3 %all-to-all-start = ((bf16[128,16,256]{0,2,1:T(8,128)(2,1)}), bf16[128,16,256]{0,2,1:T(8,128)(2,1)S(1)}, u32[]{:S(2)}, u32[]{:S(2)}) async-start(bf16[128,16,256]{0,2,1:T(8,128)(2,1)} %fusion.65), calls=%async_computation | async-start | bytes 2097152 | tf_op jit(solution)/shard_map/all_to_all | solution.py:99
  34.4 13.0 %all-to-all-done = bf16[128,16,256]{0,2,1:T(8,128)(2,1)S(1)} async-done(((bf16[128,16,256]{0,2,1:T(8,128)(2,1)}), bf16[128,16,256]{0,2,1:T(8,128)(2,1)S(1)}, u32[]{:S(2)}, u32[]{:S(2)}) %all-to-all-start) | async-done | bytes 1048608 | tf_op jit(solution)/shard_map/all_to_all | solution.py:99
  56.2 13.5 %all-to-all-done.1 = bf16[128,16,256]{0,2,1:T(8,128)(2,1)} async-done(((bf16[128,16,256]{0,2,1:T(8,128)(2,1)}), bf16[128,16,256]{0,2,1:T(8,128)(2,1)}, u32[]{:S(2)}, u32[]{:S(2)}) %all-to-all-start.1) | async-done | bytes 1048608 | tf_op jit(solution)/shard_map/all_to_all | solution.py:106
  72.9 12.3 %all-gather.5.cloned.1.call-done = bf16[2048,512]{1,0:T(8,128)(2,1)} async-done(((bf16[128,512]{1,0:T(8,128)(2,1)}), bf16[2048,512]{1,0:T(8,128)(2,1)}) %all-gather.5.cloned.1.call-update) | async-done | bytes 2097168 | tf_op jit(solution)/shard_map/all_gather | solution.py:112
  87.1 65.8 %all-gather.3.cloned.1.call-done = bf16[2048,512]{0,1:T(8,128)(2,1)} async-done(((bf16[128,512]{0,1:T(8,128)(2,1)}), bf16[2048,512]{0,1:T(8,128)(2,1)}) %all-gather.3.cloned.1.call-update) | async-done | bytes 2097168 | tf_op jit(solution)/shard_map/all_gather | solution.py:111
  158.0 268.9 %while.17 = (s32[]{:T(128)}, f32[2048,256]{0,1:T(8,128)}, f32[2048,2,128]{2,1,0:T(2,128)}, s32[2048]{0:T(1024)S(1)}, bf16[2048,128]{0,1:T(8,128)(2,1)}, /*index=...) while((s32[]{:T(128)}, f32[2048,256]{0,1:T(8,128)}, ...), condition=%wide.region_10.11_spmd, body=%wide.region_6.10_spmd.sunk | while | flops 1023352832 | bytes 38383372 | solution.py:158
  165.6 5.1 fusion.105
  170.8 5.9 convolution_bitcast_fusion.8
  183.2 6.9 %dynamic_update_slice.24 = f32[2048,256]{0,1:T(8,128)} dynamic-update-slice(f32[2048,256]{0,1:T(8,128)} %get-tuple-element.362, f32[1280,256]{0,1:T(8,128)S(1)} %maximum_add_fusion.5, s32[]{:T(128)S(6)} %min.12, s32[]{:T(128)} %constant.141.clone.1..sunk) | dynamic-update-slice | bytes 2621444 | tf_op jit(solution)/shard_map/while/body/eval_jaxpr/dynamic_update_slice | solution.py:148
  199.4 5.1 fusion.105
  204.5 5.9 convolution_bitcast_fusion.8
  217.0 6.9 %dynamic_update_slice.24 = f32[2048,256]{0,1:T(8,128)} dynamic-update-slice(f32[2048,256]{0,1:T(8,128)} %get-tuple-element.362, f32[1280,256]{0,1:T(8,128)S(1)} %maximum_add_fusion.5, s32[]{:T(128)S(6)} %min.12, s32[]{:T(128)} %constant.141.clone.1..sunk) | dynamic-update-slice | bytes 2621444 | tf_op jit(solution)/shard_map/while/body/eval_jaxpr/dynamic_update_slice | solution.py:148
  233.1 5.1 fusion.105
  238.3 5.9 convolution_bitcast_fusion.8
  250.7 6.9 %dynamic_update_slice.24 = f32[2048,256]{0,1:T(8,128)} dynamic-update-slice(f32[2048,256]{0,1:T(8,128)} %get-tuple-element.362, f32[1280,256]{0,1:T(8,128)S(1)} %maximum_add_fusion.5, s32[]{:T(128)S(6)} %min.12, s32[]{:T(128)} %constant.141.clone.1..sunk) | dynamic-update-slice | bytes 2621444 | tf_op jit(solution)/shard_map/while/body/eval_jaxpr/dynamic_update_slice | solution.py:148
  266.9 5.1 fusion.105
  272.0 5.9 convolution_bitcast_fusion.8
  284.5 6.9 %dynamic_update_slice.24 = f32[2048,256]{0,1:T(8,128)} dynamic-update-slice(f32[2048,256]{0,1:T(8,128)} %get-tuple-element.362, f32[1280,256]{0,1:T(8,128)S(1)} %maximum_add_fusion.5, s32[]{:T(128)S(6)} %min.12, s32[]{:T(128)} %constant.141.clone.1..sunk) | dynamic-update-slice | bytes 2621444 | tf_op jit(solution)/shard_map/while/body/eval_jaxpr/dynamic_update_slice | solution.py:148
  305.8 5.9 convolution_bitcast_fusion.8
  318.3 6.9 %dynamic_update_slice.24 = f32[2048,256]{0,1:T(8,128)} dynamic-update-slice(f32[2048,256]{0,1:T(8,128)} %get-tuple-element.362, f32[1280,256]{0,1:T(8,128)S(1)} %maximum_add_fusion.5, s32[]{:T(128)S(6)} %min.12, s32[]{:T(128)} %constant.141.clone.1..sunk) | dynamic-update-slice | bytes 2621444 | tf_op jit(solution)/shard_map/while/body/eval_jaxpr/dynamic_update_slice | solution.py:148
  339.5 5.9 convolution_bitcast_fusion.8
  352.0 6.7 %dynamic_update_slice.24 = f32[2048,256]{0,1:T(8,128)} dynamic-update-slice(f32[2048,256]{0,1:T(8,128)} %get-tuple-element.362, f32[1280,256]{0,1:T(8,128)S(1)} %maximum_add_fusion.5, s32[]{:T(128)S(6)} %min.12, s32[]{:T(128)} %constant.141.clone.1..sunk) | dynamic-update-slice | bytes 2621444 | tf_op jit(solution)/shard_map/while/body/eval_jaxpr/dynamic_update_slice | solution.py:148
  373.2 5.9 convolution_bitcast_fusion.8
  385.6 6.6 %dynamic_update_slice.24 = f32[2048,256]{0,1:T(8,128)} dynamic-update-slice(f32[2048,256]{0,1:T(8,128)} %get-tuple-element.362, f32[1280,256]{0,1:T(8,128)S(1)} %maximum_add_fusion.5, s32[]{:T(128)S(6)} %min.12, s32[]{:T(128)} %constant.141.clone.1..sunk) | dynamic-update-slice | bytes 2621444 | tf_op jit(solution)/shard_map/while/body/eval_jaxpr/dynamic_update_slice | solution.py:148
  406.7 5.9 convolution_bitcast_fusion.8
  419.1 6.2 dynamic_update_slice.24
  426.9 6.0 copy.156
  433.0 32.6 %all_to_all.66 = f32[2048,1,256]{2,1,0:T(1,128)} all-to-all(f32[2048,1,256]{2,1,0:T(1,128)} %copy.156), channel_id=1, replica_groups=mesh['dp'=32,'tensor'=16] {'tensor'}, dimensions={0} | all-to-all | bytes 4194304 | tf_op jit(solution)/shard_map/all_to_all | solution.py:162
  465.5 5.5 all-to-all-start.2
  484.2 15.5 %all-to-all-done.2 = f32[2048,2,128]{2,1,0:T(2,128)} async-done(((f32[2048,2,128]{2,1,0:T(2,128)}), f32[2048,2,128]{2,1,0:T(2,128)}, u32[]{:S(2)}, u32[]{:S(2)}) %all-to-all-start.2) | async-done | bytes 2097184 | tf_op jit(solution)/shard_map/all_to_all | solution.py:161
  519.3 104.3 %all-reduce = (f32[1,128]{1,0:T(1,128)S(1)}, f32[1,128]{1,0:T(1,128)S(1)}) all-reduce(f32[1,128]{1,0:T(1,128)S(1)} %bitcast.191, f32[1,128]{1,0:T(1,128)S(1)} %bitcast.192), channel_id=1, replica_groups=mesh['dp'=32,'tensor'=16] {'dp','tensor'}, use_global_device_ids=true, to_apply=%region_17.18 | all-reduce | flops 256 | bytes 2048 | tf_op jit(solution)/shard_map/psum | solution.py:170
  624.7 6.1 fusion.64
  (198 shorter events, 216.7 us)
Async XLA Ops:
  7.2 5.0 copy-start.12
  7.2 5.9 copy-start.13
  7.2 5.9 copy-start.5
  7.2 78.0 %all-gather.5.cloned.1.call-start = ((), (), s32[]{:S(2)}) async-start(), calls=%async_computation.5 | async-start | bytes 2228224 | tf_op jit(solution)/shard_map/all_gather | solution.py:112
  7.9 144.9 %all-gather.3.cloned.1.call-start = ((), (), s32[]{:S(2)}) async-start(), calls=%async_computation.4 | async-start | bytes 2228224 | tf_op jit(solution)/shard_map/all_gather | solution.py:111
  11.1 2.0 copy-start.7
  11.1 2.0 copy-start.11
  13.1 0.7 copy-start.14
  13.9 0.8 copy-start.9
  14.8 1.3 copy-start.2
  15.1 1.7 copy-start.3
  18.5 28.8 %all-to-all-start = ((bf16[128,16,256]{0,2,1:T(8,128)(2,1)}), bf16[128,16,256]{0,2,1:T(8,128)(2,1)S(1)}, u32[]{:S(2)}, u32[]{:S(2)}) async-start(bf16[128,16,256]{0,2,1:T(8,128)(2,1)} %fusion.65), calls=%async_computation | async-start | bytes 2097152 | tf_op jit(solution)/shard_map/all_to_all | solution.py:99
  28.8 2.6 copy-start.18
  47.4 22.3 %all-to-all-start.1 = ((bf16[128,16,256]{0,2,1:T(8,128)(2,1)}), bf16[128,16,256]{0,2,1:T(8,128)(2,1)}, u32[]{:S(2)}, u32[]{:S(2)}) async-start(bf16[128,16,256]{0,2,1:T(8,128)(2,1)} %multiply_convert_fusion), calls=%async_computation.1 | async-start | bytes 2097152 | tf_op jit(solution)/shard_map/all_to_all | solution.py:106
  465.5 34.1 %all-to-all-start.2 = ((f32[2048,2,128]{2,1,0:T(2,128)}), f32[2048,2,128]{2,1,0:T(2,128)}, u32[]{:S(2)}, u32[]{:S(2)}) async-start(f32[2048,2,128]{2,1,0:T(2,128)} %get-tuple-element.203), calls=%async_computation.2 | async-start | bytes 4194304 | tf_op jit(solution)/shard_map/all_to_all | solution.py:161
  474.0 2.9 copy-start.15
  499.7 5.0 copy-start.8
  510.7 2.3 copy-start
  510.7 2.3 copy-start.10
  510.7 2.3 copy-start.16
  514.3 3.1 copy-start.1
  517.4 1.9 copy-start.17
  517.4 107.3 %copy-start.6 = (bf16[128,4096]{1,0:T(8,128)(2,1)S(1)}, bf16[128,4096]{1,0:T(8,128)(2,1)}, u32[]{:S(2)}) copy-start(bf16[128,4096]{1,0:T(8,128)(2,1)} %param.10) | copy-start | bytes 3145732
  519.3 105.4 %copy-start.4 = (f32[128,4096]{1,0:T(8,128)S(1)}, f32[128,4096]{1,0:T(8,128)}, u32[]{:S(2)}) copy-start(f32[128,4096]{1,0:T(8,128)} %copy.135) | copy-start | bytes 6291460
Sparse Core Ops, SparseCore 0:
  11.3 73.8 all-gather.4
  88.9 63.8 all-gather.2
where the time goes:
time: 641 us; the launch traced here: 638 us
  matrix products  169 us (26%)
  blocking collectives  137 us (21%)
  local copies, waits for them, and re-layouts  124 us (19%)
  waiting for transfers between devices  121 us (19%)
  other arithmetic  51.5 us (8%)
  starting transfers between devices  20.8 us (3%)
  between operations  14.5 us (2%)
    psum x1, blocking collectives, local(): summed = lax.psum((q_part, k_part), ('dp', 'tensor'))  104 us
    all_gather x1, waiting for transfers between devices, local(): lax.all_gather(k_turned.reshape(tok_rows, kv_heads * HD), 'tensor', axis=...  65.8 us
    dynamic_update_slice x8, local copies, waits for them, and re-layouts, attend(): lax.dynamic_update_slice_in_dim(d_kv, lax.dynamic_slice_in_dim(d_kv, k_fi...  53.8 us
    dot_general x8, matrix products, attend(): jnp.einsum('hij,ihd->jd', d_score, q_block, preferred_element_type=jnp.fl...  47.2 us
    dot_general x8, matrix products, attend(): jnp.einsum('hij,jd->ihd', d_score, k_block, preferred_element_type=jnp.fl...  41 us
    all_to_all x1, blocking collectives, local(): lax.all_to_all(d_kv, 'tensor', split_axis=0, concat_axis=1, tiled=True)  32.6 us
    sub x8, matrix products, attend(): expo_rows = jnp.exp(scores - peak)  28.7 us
    dot_general x8, matrix products, attend(): jnp.einsum('hij,ihd->jd', prob_round, g_block, preferred_element_type=jnp...  28.3 us
  transfers between devices with their start and end apart: 5, of which 5 were waited for; matrix products, arithmetic and copies ran while one was open for 6% of the time, Pallas kernels for 0%

commit v1 on v0

v1 whole, which is shorter than its diff:
```python
import math

import jax
import jax.numpy as jnp
from jax import lax
from jax.experimental import pallas as pl
from jax.experimental.pallas import tpu as pltpu
from jax.sharding import PartitionSpec as P

HD = 128
GROUP = 8
ROWS = 128
CHIP = 2 * ROWS
BACK = 4
WIN = (BACK + 1) * CHIP
SPAN = BACK * CHIP + ROWS
PAIR = 2 * ROWS
STRIP = 16

rope_base = 1000000.0
norm_eps = 1e-06
far = -1e30
SCALE = 1.0 / math.sqrt(HD)
SCALE2 = SCALE * math.log2(math.e)
f32 = jnp.float32
bf16 = jnp.bfloat16


def unit_of(raw):
    x = raw.astype(f32)
    inv = lax.rsqrt(jnp.mean(x * x, axis=-1, keepdims=True) + norm_eps)
    return x * inv, inv


def turn(scaled, cos, sin):
    return scaled * cos + pltpu.roll(scaled, HD // 2, 1) * sin


def norm_back(d, unit, inv, gain, cos, sin):
    d_scaled = d * cos - pltpu.roll(d, HD // 2, 1) * sin
    prod = d_scaled * unit
    d_unit = d_scaled * gain
    mean = jnp.mean(prod * gain, axis=-1, keepdims=True)
    part = jnp.sum(prod.reshape(prod.shape[0] // 8, 8, HD), axis=0)
    return (d_unit - unit * mean) * inv, part


def attend_kernel(
    core_ref, q_own, g_own, rq, kv4, kv3, kv2, kv1, kv0, cos, sin, kaug, qaug, wt, qgain, kgain,
    dq_own, dq_far, dkv4, dkv3, dkv2, dkv1, dkv0, gains,
    kt, vt, qt, gt, s_a, s_b, dp_a, dp_b, p_scr, ds_scr, dk_acc, dv_acc,
):
    core = core_ref[0]
    blocks = (kv4, kv3, kv2, kv1, kv0)
    kg = kgain[...]
    qg = qgain[...]
    for i, blk in enumerate(blocks):
        rows = slice(i * CHIP, (i + 1) * CHIP)
        unit, _ = unit_of(blk[:, :HD])
        kt[rows, :HD] = turn(unit * kg, cos[rows, :], sin[rows, :]).astype(bf16)
        kt[rows, HD:] = kaug[rows, :]
        vt[rows, :] = blk[:, HD:]
    offs = []
    for j in range(2):
        b = core if j == 0 else 1 - core
        off = pl.multiple_of(b * ROWS, ROWS)
        offs.append(off)
        c = cos[pl.ds(BACK * CHIP + off, ROWS), :]
        s = sin[pl.ds(BACK * CHIP + off, ROWS), :]
        hot = qaug[pl.ds(off, ROWS), :]
        for h in range(GROUP):
            cols = slice(h * HD, (h + 1) * HD)
            rows = slice(h * ROWS, (h + 1) * ROWS)
            raw = q_own[:, cols] if j == 0 else rq[:, cols]
            unit, _ = unit_of(raw)
            qt[j, rows, :HD] = turn(unit * qg, c, s).astype(bf16)
            qt[j, rows, HD:] = hot
            if j == 0:
                gt[j, rows, :] = (g_own[:, cols].astype(f32) * wt[...]).astype(bf16)
            else:
                gt[j, rows, :] = rq[:, GROUP * HD + h * HD : GROUP * HD + (h + 1) * HD]

    dk_acc[...] = jnp.zeros_like(dk_acc)
    dv_acc[...] = jnp.zeros_like(dv_acc)
    s_buf = (s_a, s_b)
    dp_buf = (dp_a, dp_b)
    tiles = [(j, hp) for j in range(2) for hp in range(GROUP // 2)]
    causal = [
        lax.broadcasted_iota(jnp.int32, (STRIP, ROWS), 1)
        <= lax.broadcasted_iota(jnp.int32, (STRIP, ROWS), 0) + o
        for o in range(0, ROWS, STRIP)
    ]
    nt = (((1,), (1,)), ((), ()))
    tn = (((0,), (0,)), ((), ()))
    gain_rows = [jnp.zeros((8, HD), f32)]

    def scores(n):
        j, hp = tiles[n]
        rows = slice(hp * PAIR, (hp + 1) * PAIR)
        kw = kt[pl.ds(offs[j], SPAN), :]
        vw = vt[pl.ds(offs[j], SPAN), :]
        s_buf[n % 2][...] = lax.dot_general(qt[j, rows, :], kw, nt, preferred_element_type=f32)
        dp_buf[n % 2][...] = lax.dot_general(gt[j, rows, :], vw, nt, preferred_element_type=f32)

    def soft(n):
        j, hp = tiles[n]
        for r in range(0, PAIR, STRIP):
            s = s_buf[n % 2][r : r + STRIP, :]
            dp = dp_buf[n % 2][r : r + STRIP, :]
            tail = jnp.where(causal[(r % ROWS) // STRIP], s[:, SPAN - ROWS :], far)
            s = jnp.concatenate([s[:, : SPAN - ROWS], tail], axis=1)
            m = jnp.max(s, axis=-1, keepdims=True)
            e = jnp.exp2((s - m) * SCALE2)
            inv = 1.0 / jnp.sum(e, axis=-1, keepdims=True)
            delta = jnp.sum(e * dp, axis=-1, keepdims=True) * inv
            out = slice(hp * PAIR + r, hp * PAIR + r + STRIP)
            p_scr[j, out, :] = (e * inv).astype(bf16)
            ds_scr[j, out, :] = (e * (dp - delta) * (inv * SCALE)).astype(bf16)

    def grads(n):
        j, hp = tiles[n]
        rows = slice(hp * PAIR, (hp + 1) * PAIR)
        kw = kt[pl.ds(offs[j], SPAN), :HD]
        dq = lax.dot_general(ds_scr[j, rows, :], kw, (((1,), (0,)), ((), ())), preferred_element_type=f32)
        c = cos[pl.ds(BACK * CHIP + offs[j], ROWS), :]
        s = sin[pl.ds(BACK * CHIP + offs[j], ROWS), :]
        for u in range(2):
            h = hp * 2 + u
            cols = slice(h * HD, (h + 1) * HD)
            raw = q_own[:, cols] if j == 0 else rq[:, cols]
            unit, inv = unit_of(raw)
            grad, part = norm_back(dq[u * ROWS : (u + 1) * ROWS, :], unit, inv, qg, c, s)
            gain_rows[0] = gain_rows[0] + part
            if j == 0:
                dq_own[:, cols] = grad.astype(bf16)
            else:
                dq_far[:, cols] = grad.astype(bf16)
        if hp % 2 == 1:
            both = slice((hp - 1) * PAIR, (hp + 1) * PAIR)
            keys = pl.ds(offs[j], SPAN)
            dv_acc[keys, :] += lax.dot_general(p_scr[j, both, :], gt[j, both, :], tn, preferred_element_type=f32)
            dk_acc[keys, :] += lax.dot_general(ds_scr[j, both, :], qt[j, both, :HD], tn, preferred_element_type=f32)

    total = len(tiles)
    for n in range(total + 2):
        if n < total:
            scores(n)
        if 0 <= n - 1 < total:
            soft(n - 1)
        if 0 <= n - 2 < total:
            grads(n - 2)

    k_rows = jnp.zeros((8, HD), f32)
    for i, (blk, out) in enumerate(zip(blocks, (dkv4, dkv3, dkv2, dkv1, dkv0))):
        rows = slice(i * CHIP, (i + 1) * CHIP)
        unit, inv = unit_of(blk[:, :HD])
        grad, part = norm_back(dk_acc[rows, :], unit, inv, kg, cos[rows, :], sin[rows, :])
        k_rows = k_rows + part
        out[:, :HD] = grad.astype(out.dtype)
        out[:, HD:] = dv_acc[rows, :].astype(out.dtype)
    gains[:8, :] = gain_rows[0]
    gains[8:, :] = k_rows


def attend(head, core, q_states, out_grad, rq, kvs, cos, sin, kaug, qaug, wt, qgain, kgain):
    wide = GROUP * HD

    def whole(shape):
        return pl.BlockSpec(shape, lambda i, c: (0,) * len(shape))

    mine = pl.BlockSpec((ROWS, wide), lambda i, c: (0, 2 * c[0] + head))
    sds = jax.ShapeDtypeStruct
    back = sds((CHIP, 2 * HD), bf16)
    pairs = 2 * 2 * GROUP * ROWS * SPAN
    return pl.pallas_call(
        attend_kernel,
        grid_spec=pltpu.PrefetchScalarGridSpec(
            num_scalar_prefetch=1,
            grid=(1,),
            in_specs=[mine, mine, whole((ROWS, 2 * wide))]
            + [whole((CHIP, 2 * HD))] * (BACK + 1)
            + [whole((WIN, HD))] * 3
            + [whole((CHIP, HD)), whole((ROWS, 1)), whole((1, HD)), whole((1, HD))],
            out_specs=[whole((ROWS, wide))] * 2 + [whole((CHIP, 2 * HD))] * (BACK + 1) + [whole((16, HD))],
            scratch_shapes=[
                pltpu.VMEM((WIN, 2 * HD), bf16),
                pltpu.VMEM((WIN, HD), bf16),
                pltpu.VMEM((2, GROUP * ROWS, 2 * HD), bf16),
                pltpu.VMEM((2, GROUP * ROWS, HD), bf16),
                pltpu.VMEM((PAIR, SPAN), f32),
                pltpu.VMEM((PAIR, SPAN), f32),
                pltpu.VMEM((PAIR, SPAN), f32),
                pltpu.VMEM((PAIR, SPAN), f32),
                pltpu.VMEM((2, GROUP * ROWS, SPAN), bf16),
                pltpu.VMEM((2, GROUP * ROWS, SPAN), bf16),
                pltpu.VMEM((WIN, HD), f32),
                pltpu.VMEM((WIN, HD), f32),
            ],
        ),
        out_shape=[sds((ROWS, wide), bf16)] * 2 + [back] * BACK + [sds((CHIP, 2 * HD), f32), sds((16, HD), f32)],
        compiler_params=pltpu.CompilerParams(vmem_limit_bytes=40 * 2**20),
        cost_estimate=pl.CostEstimate(flops=pairs * HD * 2 * 5, bytes_accessed=4 * 2**20, transcendentals=pairs),
        name="attend_back",
    )(core, q_states, out_grad, rq, *kvs, cos, sin, kaug, qaug, wt, qgain, kgain)


def window_layout(lens, first):
    ends = jnp.cumsum(lens)
    token = first - BACK * CHIP + jnp.arange(WIN, dtype=jnp.int32)
    ended = ends[None, :] <= token[:, None]
    start = jnp.sum(jnp.where(ended, lens[None, :], 0), axis=1)
    segment = jnp.sum(ended.astype(jnp.int32), axis=1)
    owner = segment[:, None] == jnp.arange(lens.shape[0], dtype=jnp.int32)[None, :]
    length = jnp.sum(jnp.where(owner, lens[None, :], 0), axis=1)
    return jnp.where(token < 0, -1, segment), token - start, length


def local(q_states, k_states, v_states, q_gain, k_gain, out_grad, lengths, advantage):
    size = lax.axis_size("tensor")
    pos = lax.axis_index("tensor")
    core = pos % 2
    chip = pos // 2
    chips = size // 2
    group_rows = size * ROWS
    wide = GROUP * HD

    segment, position, length = window_layout(lengths[0], chip * CHIP)
    frequency = rope_base ** (-jnp.arange(HD // 2, dtype=f32) * 2.0 / HD)
    angles = position.astype(f32)[:, None] * frequency[None, :]
    c, s = jnp.cos(angles), jnp.sin(angles)
    cos = jnp.concatenate([c, c], axis=1)
    sin = jnp.concatenate([-s, s], axis=1)
    lane = jnp.arange(HD, dtype=jnp.int32)[None, :]
    same = segment[:, None] == lane
    kaug = jnp.where(same | (lane >= lengths.shape[1]), 0.0, far).astype(bf16)
    qaug = same[BACK * CHIP :].astype(bf16)
    own_len = lax.dynamic_slice_in_dim(length, BACK * CHIP + core * ROWS, ROWS, 0)
    weight = advantage.astype(f32) / 32.0 * (group_rows / lengths.shape[1]) / own_len.astype(f32)
    wt = weight[:, None]

    swap = [(t, t ^ 1) for t in range(size)]

    def heads_of(x, g, width):
        return lax.dynamic_slice_in_dim(x, g * width, width, 1)

    def half(who):
        return jnp.concatenate(
            [heads_of(y, 2 * who + g, HD) for g in range(2) for y in (k_states, v_states)], axis=1
        )

    kv_mine = half(core)
    kv_other = lax.ppermute(half(1 - core), "tensor", swap)
    first, second = (jnp.where(core == 0, a, b) for a, b in ((kv_mine, kv_other), (kv_other, kv_mine)))
    kv_chip = jnp.concatenate([first, second], axis=0)

    rqs, kvs = [], []
    for g in range(2):
        kv = kv_chip[:, g * 2 * HD : (g + 1) * 2 * HD]
        kvs.append(
            [
                lax.ppermute(kv, "tensor", [(t, t + 2 * n) for t in range(size - 2 * n)])
                for n in range(BACK, 0, -1)
            ]
            + [kv]
        )
        head = 2 * (1 - core) + g
        d_far = (heads_of(out_grad, head, wide).astype(f32) * wt).astype(bf16)
        rqs.append(
            lax.ppermute(jnp.concatenate([heads_of(q_states, head, wide), d_far], axis=1), "tensor", swap)
        )

    core_arr = core.astype(jnp.int32)[None]
    dq_mine, dq_back, dkv_sum, gain_rows = [], [], [], 0.0
    for g in range(2):
        outs = attend(
            g, core_arr, q_states, out_grad, rqs[g], kvs[g], cos, sin, kaug, qaug, wt, q_gain[None], k_gain[None]
        )
        dq_mine.append(outs[0])
        dq_back.append(lax.ppermute(outs[1], "tensor", swap))
        total = outs[2 + BACK]
        for n, part in zip(range(BACK, 0, -1), outs[2 : 2 + BACK]):
            part = lax.ppermute(part, "tensor", [(t + 2 * n, t) for t in range(size - 2 * n)])
            total = total + part.astype(f32)
        dkv_sum.append(total)
        gain_rows = gain_rows + outs[3 + BACK]

    gains = jnp.sum(gain_rows.reshape(2, 8, HD), axis=1)
    gains = jnp.pad(gains, ((0, 6), (0, 0)))
    for axis in ("tensor", "dp"):
        n = lax.axis_size(axis)
        spread = jnp.broadcast_to(gains[None], (n, 8, HD))
        gains = jnp.sum(lax.all_to_all(spread, axis, 0, 0, tiled=True), axis=0)
    gain_grad = gains[:2] / group_rows

    dkv = jnp.concatenate(dkv_sum, axis=1).astype(bf16)
    dkv_mine = lax.dynamic_slice_in_dim(dkv, core * ROWS, ROWS, 0)
    dkv_far = lax.ppermute(lax.dynamic_slice_in_dim(dkv, (1 - core) * ROWS, ROWS, 0), "tensor", swap)

    def placed(mine, other):
        return jnp.where(
            core == 0, jnp.concatenate([mine, other], axis=1), jnp.concatenate([other, mine], axis=1)
        )

    def part_of(x, which):
        return jnp.concatenate([x[:, which * HD : (which + 1) * HD], x[:, (2 + which) * HD : (3 + which) * HD]], axis=1)

    k_grad = placed(part_of(dkv_mine, 0), part_of(dkv_far, 0))
    v_grad = placed(part_of(dkv_mine, 1), part_of(dkv_far, 1))
    q_grad = placed(jnp.concatenate(dq_mine, axis=1), jnp.concatenate(dq_back, axis=1))
    return q_grad, k_grad, v_grad, gain_grad


def solution(mesh):
    return jax.shard_map(
        local,
        mesh=mesh,
        in_specs=(
            P(("dp", "tensor"), None),
            P(("dp", "tensor"), None),
            P(("dp", "tensor"), None),
            P(),
            P(),
            P(("dp", "tensor"), None),
            P("dp", None),
            P(("dp", "tensor")),
        ),
        out_specs=(
            P(("dp", "tensor"), None),
            P(("dp", "tensor"), None),
            P(("dp", "tensor"), None),
            P(),
        ),
        check_vma=False,
    )
```

time: 641 us -> 146 us (0.23)
  matrix products: 169 us -> 0 us
  blocking collectives: 137 us -> 0 us
  local copies, waits for them, and re-layouts: 124 us -> 4.86 us
  waiting for transfers between devices: 121 us -> 10.1 us
  starting transfers between devices: 20.8 us -> 81 us
  other arithmetic: 51.5 us -> 11.2 us
  Pallas kernels: 0 us -> 34.9 us
  between operations: 14.5 us -> 1.3 us
    dot_general x32 -> x0, matrix products: 140 us -> none  [the longest x8 47.2 us: attend(): jnp.einsum('hij,ihd->jd', d_score, q_block, preferred_element_type=jnp.fl...]
    psum x1 -> x0, blocking collectives: 104 us -> none  [local(): summed = lax.psum((q_part, k_part), ('dp', 'tensor'))]
    all_gather x2 -> x0, waiting for transfers between devices: 78.1 us -> none  [the longest x1 65.8 us: local(): lax.all_gather(k_turned.reshape(tok_rows, kv_heads * HD), 'tensor', axis=...]
    dynamic_update_slice x24 -> x0, local copies, waits for them, and re-layouts: 74.2 us -> none  [the longest x8 53.8 us: attend(): lax.dynamic_update_slice_in_dim(d_kv, lax.dynamic_slice_in_dim(d_kv, k_fi...]
    ppermute x0 -> x22, starting transfers between devices: none -> 50.4 us  [the longest x8 19.2 us: local(): lax.ppermute(kv, 'tensor', [(t, t + 2 * n) for t in range(size - 2 * n)])]
    all_to_all x3 -> x2, waiting for transfers between devices: 42 us -> 6.09 us  [local(): gains = jnp.sum(lax.all_to_all(spread, axis, 0, 0, tiled=True), axis=0)]
    pallas_call x0 -> x2, Pallas kernels: none -> 34.9 us  [attend(): pl.pallas_call(attend_kernel, grid_spec=pltpu.PrefetchScalarGridSpec(num_...]
    all_to_all x1 -> x0, blocking collectives: 32.6 us -> none  [local(): lax.all_to_all(d_kv, 'tensor', split_axis=0, concat_axis=1, tiled=True)]
  transfers between devices with their start and end apart: 5 -> 24, of which waited for: 5 -> 2; matrix products, arithmetic and copies ran while one was open for 6% -> 9% of each run, Pallas kernels for 0% -> 24%
where the time goes in v1:
time: 146 us; the launch traced here: 143 us
  starting transfers between devices  81 us (55%)
  Pallas kernels  34.9 us (24%)
  other arithmetic  11.2 us (8%)
  waiting for transfers between devices  10.1 us (7%)
  local copies, waits for them, and re-layouts  4.86 us (3%)
    pallas_call x2, Pallas kernels, attend(): pl.pallas_call(attend_kernel, grid_spec=pltpu.PrefetchScalarGridSpec(num_...  34.9 us
    all_to_all x2, starting transfers between devices, local(): gains = jnp.sum(lax.all_to_all(spread, axis, 0, 0, tiled=True), axis=0)  30.6 us
    ppermute x8, starting transfers between devices, local(): lax.ppermute(kv, 'tensor', [(t, t + 2 * n) for t in range(size - 2 * n)])  19.2 us
    ppermute x8, starting transfers between devices, local(): lax.ppermute(part, 'tensor', [(t + 2 * n, t) for t in range(size - 2 * n)])  10.3 us
    ppermute x1, starting transfers between devices, local(): kv_other = lax.ppermute(half(1 - core), 'tensor', swap)  8.77 us
    all_to_all x2, waiting for transfers between devices, local(): gains = jnp.sum(lax.all_to_all(spread, axis, 0, 0, tiled=True), axis=0)  6.09 us
    ppermute x2, starting transfers between devices, local(): lax.ppermute(jnp.concatenate([heads_of(q_states, head, wide), d_far], axi...  5.17 us
    ppermute x2, starting transfers between devices, local(): dq_back.append(lax.ppermute(outs[1], 'tensor', swap))  4.5 us
  transfers between devices with their start and end apart: 24, of which 2 were waited for; matrix products, arithmetic and copies ran while one was open for 9% of the time, Pallas kernels for 24%

profile of v1, /device:TPU:1, one launch (start us, length us, event | category | flops | bytes accessed | tf_op | source)
XLA Modules:
  0.0 143.3 jit_solution(65649784480878628)
XLA Ops:
  2.3 8.8 %collective-permute-start.1 = (bf16[128,512]{1,0:T(8,128)(2,1)}, bf16[128,512]{1,0:T(8,128)(2,1)S(1)}, u32[]{:S(2)}, u32[]{:S(2)}) collective-permute-start(bf16[128,512]{1,0:T(8,128)(2,1)} %pad_maximum_fusion.6), channel_id=1, source_target_pairs={{0,1},{1,0},{2,3},{3,2},{4,5},{5,4},{6,7},{7,6},{8,9},{9,8},{10,11... | collective-permute-start | bytes 393224 | tf_op jit(solution)/shard_map/ppermute | solution.py:252
  13.5 1.1 constant_dynamic-slice_fusion.9
  14.9 1.9 %collective-permute-start.6 = (bf16[128,2048]{1,0:T(8,128)(2,1)S(1)}, bf16[128,2048]{1,0:T(8,128)(2,1)S(1)}, u32[]{:S(2)}, u32[]{:S(2)}) collective-permute-start(bf16[128,2048]{1,0:T(8,128)(2,1)S(1)} %pad_maximum_fusion.3), channel_id=1, source_target_pairs={{0,1},{1,0},{2,3},{3,2},{4,5},{5,4},{6,7},{7,6},{8,9},{9,8},{10,11... | collective-permute-start | bytes 1572872 | tf_op jit(solution)/shard_map/ppermute | solution.py:269
  17.5 2.4 %fusion = (f32[1280,64]{1,0:T(8,128)S(1)}, f32[1280,64]{1,0:T(8,128)S(1)}, f32[1280,64]{1,0:T(8,128)S(1)}) fusion(f32[64]{0:T(128)S(1)} %multiply_power_fusion, f32[1280]{0:T(1024)S(1)} %subtract_convert_fusion), kind=kLoop, calls=%fused_computation.19 | loop fusion | flops 163840 | bytes 988416 | tf_op jit(solution)/shard_map/neg | solution.py:232
  20.4 1.4 collective-permute-start.10
  21.9 2.8 %collective-permute-start.7 = (bf16[256,256]{1,0:T(8,128)(2,1)S(1)}, bf16[256,256]{1,0:T(8,128)(2,1)S(1)}, u32[]{:S(2)}, u32[]{:S(2)}) collective-permute-start(bf16[256,256]{1,0:T(8,128)(2,1)S(1)} %get-tuple-element.45.kv0), channel_id=1, source_target_pairs={{0,8},{1,9},{2,10},{3,11},{4,12},{5,13},{6,14},{7,15},{16,24},{17,... | collective-permute-start | bytes 393224 | tf_op jit(solution)/shard_map/ppermute | solution.py:261
  24.7 1.3 collective-permute-start.8
  26.0 2.2 %collective-permute-start.9 = (bf16[256,256]{1,0:T(8,128)(2,1)S(1)}, bf16[256,256]{1,0:T(8,128)(2,1)S(1)}, u32[]{:S(2)}, u32[]{:S(2)}) collective-permute-start(bf16[256,256]{1,0:T(8,128)(2,1)S(1)} %get-tuple-element.45.kv0), channel_id=1, source_target_pairs={{0,4},{1,5},{2,6},{3,7},{4,8},{5,9},{6,10},{7,11},{8,12},{9,13},{1... | collective-permute-start | bytes 393224 | tf_op jit(solution)/shard_map/ppermute | solution.py:261
  28.3 3.2 %collective-permute-start = (bf16[128,2048]{1,0:T(8,128)(2,1)S(1)}, bf16[128,2048]{1,0:T(8,128)(2,1)S(1)}, u32[]{:S(2)}, u32[]{:S(2)}) collective-permute-start(bf16[128,2048]{1,0:T(8,128)(2,1)S(1)} %pad_maximum_fusion.2), channel_id=1, source_target_pairs={{0,1},{1,0},{2,3},{3,2},{4,5},{5,4},{6,7},{7,6},{8,9},{9,8},{10,11... | collective-permute-start | bytes 1572872 | tf_op jit(solution)/shard_map/ppermute | solution.py:269
  31.5 1.6 %collective-permute-start.2 = (bf16[256,256]{1,0:T(8,128)(2,1)S(1)}, bf16[256,256]{1,0:T(8,128)(2,1)S(1)}, u32[]{:S(2)}, u32[]{:S(2)}) collective-permute-start(bf16[256,256]{1,0:T(8,128)(2,1)S(1)} %get-tuple-element.44.kv0), channel_id=1, source_target_pairs={{0,8},{1,9},{2,10},{3,11},{4,12},{5,13},{6,14},{7,15},{16,24},{17,... | collective-permute-start | bytes 393224 | tf_op jit(solution)/shard_map/ppermute | solution.py:261
  33.2 3.7 %collective-permute-start.3 = (bf16[256,256]{1,0:T(8,128)(2,1)S(1)}, bf16[256,256]{1,0:T(8,128)(2,1)S(1)}, u32[]{:S(2)}, u32[]{:S(2)}) collective-permute-start(bf16[256,256]{1,0:T(8,128)(2,1)S(1)} %get-tuple-element.44.kv0), channel_id=1, source_target_pairs={{0,6},{1,7},{2,8},{3,9},{4,10},{5,11},{6,12},{7,13},{8,14},{9,15},... | collective-permute-start | bytes 393224 | tf_op jit(solution)/shard_map/ppermute | solution.py:261
  36.9 3.4 %collective-permute-start.4 = (bf16[256,256]{1,0:T(8,128)(2,1)S(1)}, bf16[256,256]{1,0:T(8,128)(2,1)S(1)}, u32[]{:S(2)}, u32[]{:S(2)}) collective-permute-start(bf16[256,256]{1,0:T(8,128)(2,1)S(1)} %get-tuple-element.44.kv0), channel_id=1, source_target_pairs={{0,4},{1,5},{2,6},{3,7},{4,8},{5,9},{6,10},{7,11},{8,12},{9,13},{1... | collective-permute-start | bytes 393224 | tf_op jit(solution)/shard_map/ppermute | solution.py:261
  40.3 2.7 %collective-permute-start.5 = (bf16[256,256]{1,0:T(8,128)(2,1)S(1)}, bf16[256,256]{1,0:T(8,128)(2,1)S(1)}, u32[]{:S(2)}, u32[]{:S(2)}) collective-permute-start(bf16[256,256]{1,0:T(8,128)(2,1)S(1)} %get-tuple-element.44.kv0), channel_id=1, source_target_pairs={{0,2},{1,3},{2,4},{3,5},{4,6},{5,7},{6,8},{7,9},{8,10},{9,11},{10,... | collective-permute-start | bytes 393224 | tf_op jit(solution)/shard_map/ppermute | solution.py:261
  43.1 17.4 %attend_back.3 = (bf16[128,1024]{1,0:T(8,128)(2,1)S(1)}, bf16[128,1024]{1,0:T(8,128)(2,1)S(1)}, bf16[256,256]{1,0:T(8,128)(2,1)S(1)}, bf16[256,256]{1,0:T(8,128)...) custom-call(s32[1]{0:T(128)} %bitcast.core_ref, ...), custom_call_target="tpu_custom_call" | custom-call | flops 6039797760 | bytes 4194304 | tf_op jit(solution)/shard_map/attend_back/pallas_call | solution.py:175
  60.5 1.3 collective-permute-start.17
  61.9 1.3 collective-permute-start.18
  63.2 1.3 collective-permute-start.19
  64.5 1.3 collective-permute-start.20
  65.8 17.5 %attend_back.2 = (bf16[128,1024]{1,0:T(8,128)(2,1)S(1)}, bf16[128,1024]{1,0:T(8,128)(2,1)S(1)}, bf16[256,256]{1,0:T(8,128)(2,1)S(1)}, bf16[256,256]{1,0:T(8,128)...) custom-call(s32[1]{0:T(128)} %bitcast.core_ref, ...), custom_call_target="tpu_custom_call" | custom-call | flops 6039797760 | bytes 4194304 | tf_op jit(solution)/shard_map/attend_back/pallas_call | solution.py:175
  85.3 15.2 %all-to-all-start = ((f32[16,8,128]{2,1,0:T(8,128)}), f32[16,8,128]{2,1,0:T(8,128)S(1)}, u32[]{:S(2)}, u32[]{:S(2)}) async-start(f32[16,8,128]{2,1,0:T(8,128)} %broadcast_in_dim.74), calls=%async_computation | async-start | bytes 131072 | tf_op jit(solution)/shard_map/all_to_all | solution.py:292
  100.5 1.3 collective-permute-start.13
  101.8 6.1 %all-to-all-done = f32[16,8,128]{2,1,0:T(8,128)S(1)} async-done(((f32[16,8,128]{2,1,0:T(8,128)}), f32[16,8,128]{2,1,0:T(8,128)S(1)}, u32[]{:S(2)}, u32[]{:S(2)}) %all-to-all-start) | async-done | bytes 65568 | tf_op jit(solution)/shard_map/all_to_all | solution.py:292
  108.5 15.4 %all-to-all-start.1 = ((f32[32,8,128]{2,1,0:T(8,128)}), f32[32,8,128]{2,1,0:T(8,128)S(1)}, u32[]{:S(2)}, u32[]{:S(2)}) async-start(f32[32,8,128]{2,1,0:T(8,128)} %broadcast_in_dim.75), calls=%async_computation.1 | async-start | bytes 262144 | tf_op jit(solution)/shard_map/all_to_all | solution.py:292
  123.9 1.3 collective-permute-start.14
  125.2 1.3 collective-permute-start.15
  126.6 1.3 collective-permute-start.16
  127.9 2.6 %collective-permute-start.11 = (bf16[128,1024]{1,0:T(8,128)(2,1)S(1)}, bf16[128,1024]{1,0:T(8,128)(2,1)S(1)}, u32[]{:S(2)}, u32[]{:S(2)}) collective-permute-start(bf16[128,1024]{1,0:T(8,128)(2,1)S(1)} %get-tuple-element.22), channel_id=1, source_target_pairs={{0,1},{1,0},{2,3},{3,2},{4,5},{5,4},{6,7},{7,6},{8,9},{9,8},{10,11... | collective-permute-start | bytes 786440 | tf_op jit(solution)/shard_map/ppermute | solution.py:279
  130.5 1.2 add_convert_fusion
  131.6 1.9 %collective-permute-start.12 = (bf16[128,1024]{1,0:T(8,128)(2,1)S(1)}, bf16[128,1024]{1,0:T(8,128)(2,1)S(1)}, u32[]{:S(2)}, u32[]{:S(2)}) collective-permute-start(bf16[128,1024]{1,0:T(8,128)(2,1)S(1)} %get-tuple-element.23), channel_id=1, source_target_pairs={{0,1},{1,0},{2,3},{3,2},{4,5},{5,4},{6,7},{7,6},{8,9},{9,8},{10,11... | collective-permute-start | bytes 786440 | tf_op jit(solution)/shard_map/ppermute | solution.py:279
  133.6 3.9 %collective-permute-done.16 = bf16[256,256]{1,0:T(8,128)(2,1)S(1)} collective-permute-done((bf16[256,256]{1,0:T(8,128)(2,1)S(1)}, bf16[256,256]{1,0:T(8,128)(2,1)S(1)}, u32[]{:S(2)}, u32[]{:S(2)}) %collective-permute-start.16) | collective-permute-done | bytes 131104 | tf_op jit(solution)/shard_map/ppermute | solution.py:282
  137.6 2.4 %collective-permute-start.21 = (bf16[128,512]{1,0:T(8,128)(2,1)S(1)}, bf16[128,512]{1,0:T(8,128)(2,1)S(1)}, u32[]{:S(2)}, u32[]{:S(2)}) collective-permute-start(bf16[128,512]{1,0:T(8,128)(2,1)S(1)} %get-tuple-element.43), channel_id=1, source_target_pairs={{0,1},{1,0},{2,3},{3,2},{4,5},{5,4},{6,7},{7,6},{8,9},{9,8},{10,11... | collective-permute-start | bytes 393224 | tf_op jit(solution)/shard_map/ppermute | solution.py:297
  140.1 1.2 maximum_select_fusion
  (70 shorter events, 10.3 us)
Async XLA Ops:
  0.6 14.0 %copy-start.6 = (s32[128]{0:T(128)S(1)}, s32[128]{0:T(128)}, u32[]{:S(2)}) copy-start(s32[128]{0:T(128)} %param.15) | copy-start | bytes 1540
  0.6 14.0 %copy-start.1 = (bf16[128,4096]{1,0:T(8,128)(2,1)S(1)}, bf16[128,4096]{1,0:T(8,128)(2,1)}, u32[]{:S(2)}) copy-start(bf16[128,4096]{1,0:T(8,128)(2,1)} %g_own.3) | copy-start | bytes 3145732
  2.3 18.0 %collective-permute-start.1 = (bf16[128,512]{1,0:T(8,128)(2,1)}, bf16[128,512]{1,0:T(8,128)(2,1)S(1)}, u32[]{:S(2)}, u32[]{:S(2)}) collective-permute-start(bf16[128,512]{1,0:T(8,128)(2,1)} %pad_maximum_fusion.6), channel_id=1, source_target_pairs={{0,1},{1,0},{2,3},{3,2},{4,5},{5,4},{6,7},{7,6},{8,9},{9,8},{10,11... | collective-permute-start | bytes 393224 | tf_op jit(solution)/shard_map/ppermute | solution.py:252
  14.9 25.4 %collective-permute-start.6 = (bf16[128,2048]{1,0:T(8,128)(2,1)S(1)}, bf16[128,2048]{1,0:T(8,128)(2,1)S(1)}, u32[]{:S(2)}, u32[]{:S(2)}) collective-permute-start(bf16[128,2048]{1,0:T(8,128)(2,1)S(1)} %pad_maximum_fusion.3), channel_id=1, source_target_pairs={{0,1},{1,0},{2,3},{3,2},{4,5},{5,4},{6,7},{7,6},{8,9},{9,8},{10,11... | collective-permute-start | bytes 1572872 | tf_op jit(solution)/shard_map/ppermute | solution.py:269
  20.3 22.8 %copy-start = (bf16[128,4096]{1,0:T(8,128)(2,1)S(1)}, bf16[128,4096]{1,0:T(8,128)(2,1)}, u32[]{:S(2)}) copy-start(bf16[128,4096]{1,0:T(8,128)(2,1)} %q_own.3) | copy-start | bytes 3145732
  20.3 22.8 %copy-start.4 = (f32[128]{0:T(128)S(1)}, f32[128]{0:T(128)}, u32[]{:S(2)}) copy-start(f32[128]{0:T(128)} %param.11) | copy-start | bytes 1540
  20.3 22.8 %copy-start.5 = (f32[128]{0:T(128)S(1)}, f32[128]{0:T(128)}, u32[]{:S(2)}) copy-start(f32[128]{0:T(128)} %param.12) | copy-start | bytes 1540
  20.4 7.8 %collective-permute-start.10 = (bf16[256,256]{1,0:T(8,128)(2,1)S(1)}, bf16[256,256]{1,0:T(8,128)(2,1)S(1)}, u32[]{:S(2)}, u32[]{:S(2)}) collective-permute-start(bf16[256,256]{1,0:T(8,128)(2,1)S(1)} %get-tuple-element.45.kv0), channel_id=1, source_target_pairs={{0,2},{1,3},{2,4},{3,5},{4,6},{5,7},{6,8},{7,9},{8,10},{9,11},{10,... | collective-permute-start | bytes 393224 | tf_op jit(solution)/shard_map/ppermute | solution.py:261
  21.9 9.6 %collective-permute-start.7 = (bf16[256,256]{1,0:T(8,128)(2,1)S(1)}, bf16[256,256]{1,0:T(8,128)(2,1)S(1)}, u32[]{:S(2)}, u32[]{:S(2)}) collective-permute-start(bf16[256,256]{1,0:T(8,128)(2,1)S(1)} %get-tuple-element.45.kv0), channel_id=1, source_target_pairs={{0,8},{1,9},{2,10},{3,11},{4,12},{5,13},{6,14},{7,15},{16,24},{17,... | collective-permute-start | bytes 393224 | tf_op jit(solution)/shard_map/ppermute | solution.py:261
  24.7 8.5 %collective-permute-start.8 = (bf16[256,256]{1,0:T(8,128)(2,1)S(1)}, bf16[256,256]{1,0:T(8,128)(2,1)S(1)}, u32[]{:S(2)}, u32[]{:S(2)}) collective-permute-start(bf16[256,256]{1,0:T(8,128)(2,1)S(1)} %get-tuple-element.45.kv0), channel_id=1, source_target_pairs={{0,6},{1,7},{2,8},{3,9},{4,10},{5,11},{6,12},{7,13},{8,14},{9,15},... | collective-permute-start | bytes 393224 | tf_op jit(solution)/shard_map/ppermute | solution.py:261
  26.0 10.9 %collective-permute-start.9 = (bf16[256,256]{1,0:T(8,128)(2,1)S(1)}, bf16[256,256]{1,0:T(8,128)(2,1)S(1)}, u32[]{:S(2)}, u32[]{:S(2)}) collective-permute-start(bf16[256,256]{1,0:T(8,128)(2,1)S(1)} %get-tuple-element.45.kv0), channel_id=1, source_target_pairs={{0,4},{1,5},{2,6},{3,7},{4,8},{5,9},{6,10},{7,11},{8,12},{9,13},{1... | collective-permute-start | bytes 393224 | tf_op jit(solution)/shard_map/ppermute | solution.py:261
  28.3 37.5 %collective-permute-start = (bf16[128,2048]{1,0:T(8,128)(2,1)S(1)}, bf16[128,2048]{1,0:T(8,128)(2,1)S(1)}, u32[]{:S(2)}, u32[]{:S(2)}) collective-permute-start(bf16[128,2048]{1,0:T(8,128)(2,1)S(1)} %pad_maximum_fusion.2), channel_id=1, source_target_pairs={{0,1},{1,0},{2,3},{3,2},{4,5},{5,4},{6,7},{7,6},{8,9},{9,8},{10,11... | collective-permute-start | bytes 1572872 | tf_op jit(solution)/shard_map/ppermute | solution.py:269
  31.5 29.0 %collective-permute-start.2 = (bf16[256,256]{1,0:T(8,128)(2,1)S(1)}, bf16[256,256]{1,0:T(8,128)(2,1)S(1)}, u32[]{:S(2)}, u32[]{:S(2)}) collective-permute-start(bf16[256,256]{1,0:T(8,128)(2,1)S(1)} %get-tuple-element.44.kv0), channel_id=1, source_target_pairs={{0,8},{1,9},{2,10},{3,11},{4,12},{5,13},{6,14},{7,15},{16,24},{17,... | collective-permute-start | bytes 393224 | tf_op jit(solution)/shard_map/ppermute | solution.py:261
  33.2 28.7 %collective-permute-start.3 = (bf16[256,256]{1,0:T(8,128)(2,1)S(1)}, bf16[256,256]{1,0:T(8,128)(2,1)S(1)}, u32[]{:S(2)}, u32[]{:S(2)}) collective-permute-start(bf16[256,256]{1,0:T(8,128)(2,1)S(1)} %get-tuple-element.44.kv0), channel_id=1, source_target_pairs={{0,6},{1,7},{2,8},{3,9},{4,10},{5,11},{6,12},{7,13},{8,14},{9,15},... | collective-permute-start | bytes 393224 | tf_op jit(solution)/shard_map/ppermute | solution.py:261
  36.9 26.3 %collective-permute-start.4 = (bf16[256,256]{1,0:T(8,128)(2,1)S(1)}, bf16[256,256]{1,0:T(8,128)(2,1)S(1)}, u32[]{:S(2)}, u32[]{:S(2)}) collective-permute-start(bf16[256,256]{1,0:T(8,128)(2,1)S(1)} %get-tuple-element.44.kv0), channel_id=1, source_target_pairs={{0,4},{1,5},{2,6},{3,7},{4,8},{5,9},{6,10},{7,11},{8,12},{9,13},{1... | collective-permute-start | bytes 393224 | tf_op jit(solution)/shard_map/ppermute | solution.py:261
  40.3 24.1 %collective-permute-start.5 = (bf16[256,256]{1,0:T(8,128)(2,1)S(1)}, bf16[256,256]{1,0:T(8,128)(2,1)S(1)}, u32[]{:S(2)}, u32[]{:S(2)}) collective-permute-start(bf16[256,256]{1,0:T(8,128)(2,1)S(1)} %get-tuple-element.44.kv0), channel_id=1, source_target_pairs={{0,2},{1,3},{2,4},{3,5},{4,6},{5,7},{6,8},{7,9},{8,10},{9,11},{10,... | collective-permute-start | bytes 393224 | tf_op jit(solution)/shard_map/ppermute | solution.py:261
  60.5 63.4 %collective-permute-start.17 = (bf16[256,256]{1,0:T(8,128)(2,1)S(1)}, bf16[256,256]{1,0:T(8,128)(2,1)}, u32[]{:S(2)}, u32[]{:S(2)}) collective-permute-start(bf16[256,256]{1,0:T(8,128)(2,1)S(1)} %get-tuple-element.30), channel_id=1, source_target_pairs={{8,0},{9,1},{10,2},{11,3},{12,4},{13,5},{14,6},{15,7},{24,16},{25,... | collective-permute-start | bytes 393224 | tf_op jit(solution)/shard_map/ppermute | solution.py:282
  61.9 63.4 %collective-permute-start.18 = (bf16[256,256]{1,0:T(8,128)(2,1)S(1)}, bf16[256,256]{1,0:T(8,128)(2,1)}, u32[]{:S(2)}, u32[]{:S(2)}) collective-permute-start(bf16[256,256]{1,0:T(8,128)(2,1)S(1)} %get-tuple-element.31), channel_id=1, source_target_pairs={{6,0},{7,1},{8,2},{9,3},{10,4},{11,5},{12,6},{13,7},{14,8},{15,9},... | collective-permute-start | bytes 393224 | tf_op jit(solution)/shard_map/ppermute | solution.py:282
  63.2 63.4 %collective-permute-start.19 = (bf16[256,256]{1,0:T(8,128)(2,1)S(1)}, bf16[256,256]{1,0:T(8,128)(2,1)}, u32[]{:S(2)}, u32[]{:S(2)}) collective-permute-start(bf16[256,256]{1,0:T(8,128)(2,1)S(1)} %get-tuple-element.32), channel_id=1, source_target_pairs={{4,0},{5,1},{6,2},{7,3},{8,4},{9,5},{10,6},{11,7},{12,8},{13,9},{1... | collective-permute-start | bytes 393224 | tf_op jit(solution)/shard_map/ppermute | solution.py:282
  64.5 63.4 %collective-permute-start.20 = (bf16[256,256]{1,0:T(8,128)(2,1)S(1)}, bf16[256,256]{1,0:T(8,128)(2,1)}, u32[]{:S(2)}, u32[]{:S(2)}) collective-permute-start(bf16[256,256]{1,0:T(8,128)(2,1)S(1)} %get-tuple-element.33), channel_id=1, source_target_pairs={{2,0},{3,1},{4,2},{5,3},{6,4},{7,5},{8,6},{9,7},{10,8},{11,9},{12,... | collective-permute-start | bytes 393224 | tf_op jit(solution)/shard_map/ppermute | solution.py:282
  83.3 0.7 copy-start.2
  84.0 0.7 copy-start.3
  85.3 22.6 %all-to-all-start = ((f32[16,8,128]{2,1,0:T(8,128)}), f32[16,8,128]{2,1,0:T(8,128)S(1)}, u32[]{:S(2)}, u32[]{:S(2)}) async-start(f32[16,8,128]{2,1,0:T(8,128)} %broadcast_in_dim.74), calls=%async_computation | async-start | bytes 131072 | tf_op jit(solution)/shard_map/all_to_all | solution.py:292
  100.5 31.2 %collective-permute-start.13 = (bf16[256,256]{1,0:T(8,128)(2,1)}, bf16[256,256]{1,0:T(8,128)(2,1)S(1)}, u32[]{:S(2)}, u32[]{:S(2)}) collective-permute-start(bf16[256,256]{1,0:T(8,128)(2,1)} %copy-done.3), channel_id=1, source_target_pairs={{8,0},{9,1},{10,2},{11,3},{12,4},{13,5},{14,6},{15,7},{24,16},{25,... | collective-permute-start | bytes 393224 | tf_op jit(solution)/shard_map/ppermute | solution.py:282
  108.5 34.2 %all-to-all-start.1 = ((f32[32,8,128]{2,1,0:T(8,128)}), f32[32,8,128]{2,1,0:T(8,128)S(1)}, u32[]{:S(2)}, u32[]{:S(2)}) async-start(f32[32,8,128]{2,1,0:T(8,128)} %broadcast_in_dim.75), calls=%async_computation.1 | async-start | bytes 262144 | tf_op jit(solution)/shard_map/all_to_all | solution.py:292
  123.9 9.6 %collective-permute-start.14 = (bf16[256,256]{1,0:T(8,128)(2,1)}, bf16[256,256]{1,0:T(8,128)(2,1)S(1)}, u32[]{:S(2)}, u32[]{:S(2)}) collective-permute-start(bf16[256,256]{1,0:T(8,128)(2,1)} %copy-done.2), channel_id=1, source_target_pairs={{6,0},{7,1},{8,2},{9,3},{10,4},{11,5},{12,6},{13,7},{14,8},{15,9},... | collective-permute-start | bytes 393224 | tf_op jit(solution)/shard_map/ppermute | solution.py:282
  125.2 8.3 %collective-permute-start.15 = (bf16[256,256]{1,0:T(8,128)(2,1)S(1)}, bf16[256,256]{1,0:T(8,128)(2,1)S(1)}, u32[]{:S(2)}, u32[]{:S(2)}) collective-permute-start(bf16[256,256]{1,0:T(8,128)(2,1)S(1)} %get-tuple-element.27), channel_id=1, source_target_pairs={{4,0},{5,1},{6,2},{7,3},{8,4},{9,5},{10,6},{11,7},{12,8},{13,9},{1... | collective-permute-start | bytes 393224 | tf_op jit(solution)/shard_map/ppermute | solution.py:282
  126.6 10.9 %collective-permute-start.16 = (bf16[256,256]{1,0:T(8,128)(2,1)S(1)}, bf16[256,256]{1,0:T(8,128)(2,1)S(1)}, u32[]{:S(2)}, u32[]{:S(2)}) collective-permute-start(bf16[256,256]{1,0:T(8,128)(2,1)S(1)} %get-tuple-element.28), channel_id=1, source_target_pairs={{2,0},{3,1},{4,2},{5,3},{6,4},{7,5},{8,6},{9,7},{10,8},{11,9},{12,... | collective-permute-start | bytes 393224 | tf_op jit(solution)/shard_map/ppermute | solution.py:282
  127.9 12.2 %collective-permute-start.11 = (bf16[128,1024]{1,0:T(8,128)(2,1)S(1)}, bf16[128,1024]{1,0:T(8,128)(2,1)S(1)}, u32[]{:S(2)}, u32[]{:S(2)}) collective-permute-start(bf16[128,1024]{1,0:T(8,128)(2,1)S(1)} %get-tuple-element.22), channel_id=1, source_target_pairs={{0,1},{1,0},{2,3},{3,2},{4,5},{5,4},{6,7},{7,6},{8,9},{9,8},{10,11... | collective-permute-start | bytes 786440 | tf_op jit(solution)/shard_map/ppermute | solution.py:279
  131.6 8.4 %collective-permute-start.12 = (bf16[128,1024]{1,0:T(8,128)(2,1)S(1)}, bf16[128,1024]{1,0:T(8,128)(2,1)S(1)}, u32[]{:S(2)}, u32[]{:S(2)}) collective-permute-start(bf16[128,1024]{1,0:T(8,128)(2,1)S(1)} %get-tuple-element.23), channel_id=1, source_target_pairs={{0,1},{1,0},{2,3},{3,2},{4,5},{5,4},{6,7},{7,6},{8,9},{9,8},{10,11... | collective-permute-start | bytes 786440 | tf_op jit(solution)/shard_map/ppermute | solution.py:279
  137.6 3.7 %collective-permute-start.21 = (bf16[128,512]{1,0:T(8,128)(2,1)S(1)}, bf16[128,512]{1,0:T(8,128)(2,1)S(1)}, u32[]{:S(2)}, u32[]{:S(2)}) collective-permute-start(bf16[128,512]{1,0:T(8,128)(2,1)S(1)} %get-tuple-element.43), channel_id=1, source_target_pairs={{0,1},{1,0},{2,3},{3,2},{4,5},{5,4},{6,7},{7,6},{8,9},{9,8},{10,11... | collective-permute-start | bytes 393224 | tf_op jit(solution)/shard_map/ppermute | solution.py:297

commit v2 on v1

v2 whole, which is shorter than its diff:
```python
import math

import jax
import jax.numpy as jnp
from jax import lax
from jax.experimental import pallas as pl
from jax.experimental.pallas import tpu as pltpu
from jax.sharding import PartitionSpec as P

HD = 128
GROUP = 8
ROWS = 128
CHIP = 2 * ROWS
HEADS = 2
BACK = 4
WIN = (BACK + 1) * CHIP
SPAN = BACK * CHIP + ROWS
PART = SPAN // 3
SUB = 64
PAIR = 2 * ROWS

rope_base = 1000000.0
norm_eps = 1e-06
far = -1e30
SCALE = 1.0 / math.sqrt(HD)
SCALE2 = SCALE * math.log2(math.e)
f32 = jnp.float32
bf16 = jnp.bfloat16


def unit_of(raw):
    x = raw.astype(f32)
    inv = lax.rsqrt(jnp.mean(x * x, axis=-1, keepdims=True) + norm_eps)
    return x * inv, inv


def turn(scaled, cos, sin):
    return scaled * cos + pltpu.roll(scaled, HD // 2, 1) * sin


def norm_back(d, unit, inv, gain, cos, sin):
    d_scaled = d * cos - pltpu.roll(d, HD // 2, 1) * sin
    prod = d_scaled * unit
    d_unit = d_scaled * gain
    mean = jnp.mean(prod * gain, axis=-1, keepdims=True)
    part = jnp.sum(prod.reshape(prod.shape[0] // 8, 8, HD), axis=0)
    return (d_unit - unit * mean) * inv, part


def attend_kernel(
    core_ref, q_own, g_own, rq, kv_far, kv2, kv1, kv0, cos, sin, kaug, qaug, wt, qgain, kgain,
    dq_own, dq_far, dkv4, dkv3, dkv2, dkv1, dkv0, gains,
    kt, vt, qt, gt, s_buf, dp_buf, p_scr, ds_scr, dk_acc, dv_acc,
):
    core = core_ref[0]
    blocks = (kv_far.at[:CHIP], kv_far.at[CHIP:], kv2, kv1, kv0)
    d_blocks = (dkv4, dkv3, dkv2, dkv1, dkv0)
    kg = kgain[...]
    qg = qgain[...]
    for i, blk in enumerate(blocks):
        rows = slice(i * CHIP, (i + 1) * CHIP)
        unit, _ = unit_of(blk[:, :HD])
        kt[rows, :HD] = turn(unit * kg, cos[rows, :], sin[rows, :]).astype(bf16)
        kt[rows, HD:] = kaug[rows, :]
        vt[rows, :] = blk[:, HD:]
    offs = []
    for j in range(2):
        b = core if j == 0 else 1 - core
        off = pl.multiple_of(b * ROWS, ROWS)
        offs.append(off)
        c = cos[pl.ds(BACK * CHIP + off, ROWS), :]
        s = sin[pl.ds(BACK * CHIP + off, ROWS), :]
        hot = qaug[pl.ds(off, ROWS), :]
        for h in range(GROUP):
            cols = slice(h * HD, (h + 1) * HD)
            rows = slice(h * ROWS, (h + 1) * ROWS)
            raw = q_own[:, cols] if j == 0 else rq[:, cols]
            unit, _ = unit_of(raw)
            qt[j, rows, :HD] = turn(unit * qg, c, s).astype(bf16)
            qt[j, rows, HD:] = hot
            if j == 0:
                gt[j, rows, :] = (g_own[:, cols].astype(f32) * wt[...]).astype(bf16)
            else:
                gt[j, rows, :] = rq[:, GROUP * HD + h * HD : GROUP * HD + (h + 1) * HD]

    dk_acc[...] = jnp.zeros_like(dk_acc)
    dv_acc[...] = jnp.zeros_like(dv_acc)
    tiles = [(j, hp) for j in range(2) for hp in range(GROUP // 2)]
    total = len(tiles)
    chunks = SPAN // PART
    nt = (((1,), (1,)), ((), ()))
    tn = (((0,), (0,)), ((), ()))
    nn = (((1,), (0,)), ((), ()))
    key_row = lax.broadcasted_iota(jnp.int32, (ROWS, PAIR), 0)
    query = lax.broadcasted_iota(jnp.int32, (ROWS, PAIR), 1) % ROWS
    causal = key_row <= query
    gain_rows = [jnp.zeros((8, HD), f32)]
    peaks, sums, dots, shift, delta = {}, {}, {}, {}, {}

    def fold(x, op):
        out = x[:8]
        for r in range(8, x.shape[0], 8):
            out = op(out, x[r : r + 8])
        return out

    def cols_of(n):
        hp = tiles[n][1]
        return slice(hp * PAIR, (hp + 1) * PAIR)

    def keys_of(n, c):
        return pl.ds(pl.multiple_of(offs[tiles[n][0]] + c * PART, ROWS), PART)

    def scores(n, c):
        j = tiles[n][0]
        here = slice(c * PART, (c + 1) * PART)
        s = lax.dot_general(kt[keys_of(n, c), :], qt[j, cols_of(n), :], nt, preferred_element_type=f32)
        if c == chunks - 1:
            s = jnp.concatenate([s[: PART - ROWS], jnp.where(causal, s[PART - ROWS :], far)], axis=0)
        s_buf[n % 3, here, :] = s
        top = fold(s, jnp.maximum)
        peaks[n] = jnp.maximum(peaks[n], top) if c else top
        dp_buf[n % 3, here, :] = lax.dot_general(
            vt[keys_of(n, c), :], gt[j, cols_of(n), :], nt, preferred_element_type=f32
        )

    def weights(n, c):
        if c == 0:
            shift[n] = jnp.max(peaks[n], axis=0, keepdims=True) * SCALE2
            sums[n] = dots[n] = 0.0
        for r in range(c * PART, (c + 1) * PART, SUB):
            e = jnp.exp2(s_buf[n % 3, r : r + SUB, :] * SCALE2 - shift[n])
            sums[n] = sums[n] + fold(e, jnp.add)
            dots[n] = dots[n] + fold(e * dp_buf[n % 3, r : r + SUB, :], jnp.add)

    def slopes(n, c):
        if c == 0:
            norm = jnp.sum(sums[n], axis=0, keepdims=True)
            delta[n] = jnp.sum(dots[n], axis=0, keepdims=True) / norm
            shift[n] = shift[n] + jnp.log2(norm)
        j = tiles[n][0]
        for r in range(c * PART, (c + 1) * PART, SUB):
            p = jnp.exp2(s_buf[n % 3, r : r + SUB, :] * SCALE2 - shift[n])
            p_scr[j, r : r + SUB, cols_of(n)] = p.astype(bf16)
            ds_scr[j, r : r + SUB, cols_of(n)] = (p * (dp_buf[n % 3, r : r + SUB, :] - delta[n]) * SCALE).astype(bf16)

    def query_grads(n):
        j, hp = tiles[n]
        kw = kt[pl.ds(offs[j], SPAN), :HD]
        dq = lax.dot_general(ds_scr[j, :, cols_of(n)], kw, tn, preferred_element_type=f32)
        c = cos[pl.ds(BACK * CHIP + offs[j], ROWS), :]
        s = sin[pl.ds(BACK * CHIP + offs[j], ROWS), :]
        for u in range(2):
            h = hp * 2 + u
            cols = slice(h * HD, (h + 1) * HD)
            raw = q_own[:, cols] if j == 0 else rq[:, cols]
            unit, inv = unit_of(raw)
            grad, part = norm_back(dq[u * ROWS : (u + 1) * ROWS, :], unit, inv, qg, c, s)
            gain_rows[0] = gain_rows[0] + part
            if j == 0:
                dq_own[:, cols] = grad.astype(bf16)
            else:
                dq_far[:, cols] = grad.astype(bf16)

    def key_grads(n, c):
        j, hp = tiles[n]
        both = slice((hp - 1) * PAIR, (hp + 1) * PAIR)
        here = slice(c * PART, (c + 1) * PART)
        keys = keys_of(n, c)
        dv_acc[keys, :] += lax.dot_general(p_scr[j, here, both], gt[j, both, :], nn, preferred_element_type=f32)
        dk_acc[keys, :] += lax.dot_general(ds_scr[j, here, both], qt[j, both, :HD], nn, preferred_element_type=f32)

    for step in range(total + 3):
        for c in range(chunks):
            if step < total:
                scores(step, c)
            if 0 <= step - 1 < total:
                weights(step - 1, c)
            if 0 <= step - 2 < total:
                slopes(step - 2, c)
            n = step - 3
            if 0 <= n < total and n % 2 == 1:
                key_grads(n, c)
        if 0 <= step - 3 < total:
            query_grads(step - 3)

    k_rows = jnp.zeros((8, HD), f32)
    for i, (blk, out) in enumerate(zip(blocks, d_blocks)):
        rows = slice(i * CHIP, (i + 1) * CHIP)
        unit, inv = unit_of(blk[:, :HD])
        grad, part = norm_back(dk_acc[rows, :], unit, inv, kg, cos[rows, :], sin[rows, :])
        k_rows = k_rows + part
        out[:, :HD] = grad.astype(out.dtype)
        out[:, HD:] = dv_acc[rows, :].astype(out.dtype)
    rows = jnp.concatenate([gain_rows[0], k_rows], axis=0)
    begun = pl.program_id(0) > 0
    gains[...] = rows + jnp.where(begun, gains[...], 0.0)


def attend(core, q_states, out_grad, rq, kvs, cos, sin, kaug, qaug, wt, qgain, kgain):
    wide = GROUP * HD

    def whole(shape):
        return pl.BlockSpec(shape, lambda g, c: (0,) * len(shape))

    def column(shape):
        return pl.BlockSpec(shape, lambda g, c: (0, g))

    mine = pl.BlockSpec((ROWS, wide), lambda g, c: (0, 2 * c[0] + g))
    sds = jax.ShapeDtypeStruct
    pairs = HEADS * 2 * GROUP * ROWS * SPAN
    return pl.pallas_call(
        attend_kernel,
        grid_spec=pltpu.PrefetchScalarGridSpec(
            num_scalar_prefetch=1,
            grid=(HEADS,),
            in_specs=[mine, mine, column((ROWS, 2 * wide))]
            + [column((2 * CHIP, 2 * HD))] + [column((CHIP, 2 * HD))] * 3
            + [whole((WIN, HD))] * 3
            + [whole((CHIP, HD)), whole((ROWS, 1)), whole((1, HD)), whole((1, HD))],
            out_specs=[column((ROWS, wide))] * 2
            + [column((CHIP, 2 * HD))] * (BACK + 1)
            + [whole((16, HD))],
            scratch_shapes=[
                pltpu.VMEM((WIN, 2 * HD), bf16),
                pltpu.VMEM((WIN, HD), bf16),
                pltpu.VMEM((2, GROUP * ROWS, 2 * HD), bf16),
                pltpu.VMEM((2, GROUP * ROWS, HD), bf16),
                pltpu.VMEM((3, SPAN, PAIR), f32),
                pltpu.VMEM((3, SPAN, PAIR), f32),
                pltpu.VMEM((2, SPAN, GROUP * ROWS), bf16),
                pltpu.VMEM((2, SPAN, GROUP * ROWS), bf16),
                pltpu.VMEM((WIN, HD), f32),
                pltpu.VMEM((WIN, HD), f32),
            ],
        ),
        out_shape=[sds((ROWS, HEADS * wide), bf16)] * 2
        + [sds((CHIP, HEADS * 2 * HD), bf16)] * BACK
        + [sds((CHIP, HEADS * 2 * HD), f32), sds((16, HD), f32)],
        compiler_params=pltpu.CompilerParams(vmem_limit_bytes=58 * 2**20),
        cost_estimate=pl.CostEstimate(flops=pairs * HD * 2 * 5, bytes_accessed=4 * 2**20, transcendentals=pairs),
        name="attend_back",
    )(core, q_states, out_grad, rq, *kvs, cos, sin, kaug, qaug, wt, qgain, kgain)


def window_layout(lens, first):
    ends = jnp.cumsum(lens)
    token = first - BACK * CHIP + jnp.arange(WIN, dtype=jnp.int32)
    ended = ends[None, :] <= token[:, None]
    start = jnp.sum(jnp.where(ended, lens[None, :], 0), axis=1)
    segment = jnp.sum(ended.astype(jnp.int32), axis=1)
    owner = segment[:, None] == jnp.arange(lens.shape[0], dtype=jnp.int32)[None, :]
    length = jnp.sum(jnp.where(owner, lens[None, :], 0), axis=1)
    return jnp.where(token < 0, -1, segment), token - start, length


def local(q_states, k_states, v_states, q_gain, k_gain, out_grad, lengths, advantage):
    size = lax.axis_size("tensor")
    pos = lax.axis_index("tensor")
    core = pos % 2
    chip = pos // 2
    chips = size // 2
    group_rows = size * ROWS
    wide = GROUP * HD

    swap = [(t, t ^ 1) for t in range(size)]

    def heads_of(x, g, width):
        return lax.dynamic_slice_in_dim(x, g * width, width, 1)

    def half(who):
        return jnp.concatenate(
            [heads_of(y, HEADS * who + g, HD) for g in range(HEADS) for y in (k_states, v_states)], axis=1
        )

    kv_mine = half(core)
    kv_other = lax.ppermute(half(1 - core), "tensor", swap)
    first, second = (jnp.where(core == 0, a, b) for a, b in ((kv_mine, kv_other), (kv_other, kv_mine)))
    kv_chip = jnp.concatenate([first, second], axis=0)
    kv_chip, lens, q_states, out_grad = lax.optimization_barrier((kv_chip, lengths[0], q_states, out_grad))
    def later(x, n):
        return lax.ppermute(x, "tensor", [(t, t + 2 * n) for t in range(size - 2 * n)])

    kv1, kv2 = later(kv_chip, 1), later(kv_chip, 2)
    kvs = [later(jnp.concatenate([kv2, kv1], axis=0), 2), kv2, kv1, kv_chip]

    segment, position, length = window_layout(lens, chip * CHIP)
    frequency = rope_base ** (-jnp.arange(HD // 2, dtype=f32) * 2.0 / HD)
    angles = position.astype(f32)[:, None] * frequency[None, :]
    c, s = jnp.cos(angles), jnp.sin(angles)
    cos = jnp.concatenate([c, c], axis=1)
    sin = jnp.concatenate([-s, s], axis=1)
    lane = jnp.arange(HD, dtype=jnp.int32)[None, :]
    same = segment[:, None] == lane
    kaug = jnp.where(same | (lane >= lengths.shape[1]), 0.0, far).astype(bf16)
    qaug = same[BACK * CHIP :].astype(bf16)
    own_len = lax.dynamic_slice_in_dim(length, BACK * CHIP + core * ROWS, ROWS, 0)
    weight = advantage.astype(f32) / 32.0 * (group_rows / lengths.shape[1]) / own_len.astype(f32)
    wt = weight[:, None]

    pieces = []
    for g in range(HEADS):
        head = HEADS * (1 - core) + g
        pieces += [heads_of(q_states, head, wide), (heads_of(out_grad, head, wide).astype(f32) * wt).astype(bf16)]
    rq = lax.ppermute(jnp.concatenate(pieces, axis=1), "tensor", swap)

    outs = attend(
        core.astype(jnp.int32)[None], q_states, out_grad, rq, kvs, cos, sin, kaug, qaug, wt, q_gain[None], k_gain[None]
    )
    dq_mine, dq_far, *parts, dkv, gain_rows = outs

    gains = jnp.sum(gain_rows.reshape(2, 8, HD), axis=1)
    gains = gains.reshape(1, 2 * HD)

    def gathered_sum(x, axis):
        n = lax.axis_size(axis)
        spread = jnp.broadcast_to(x[None], (n, 1, 2 * HD))
        return jnp.sum(lax.all_to_all(spread, axis, 0, 0, tiled=True), axis=0)

    dq_back = lax.ppermute(dq_far, "tensor", swap)

    def earlier(x, n):
        return lax.ppermute(x, "tensor", [(t + 2 * n, t) for t in range(size - 2 * n)])

    back = [earlier(part, n) for n, part in zip(range(BACK, 0, -1), parts)]
    gains, back = lax.optimization_barrier((gathered_sum(gains, "dp"), back))
    gain_grad = gathered_sum(gains, "tensor").reshape(2, HD) / group_rows
    for part in back:
        dkv = dkv + part.astype(f32)
    dkv = dkv.astype(bf16)
    dkv_mine = lax.dynamic_slice_in_dim(dkv, core * ROWS, ROWS, 0)
    dkv_far = lax.ppermute(lax.dynamic_slice_in_dim(dkv, (1 - core) * ROWS, ROWS, 0), "tensor", swap)

    def placed(mine, other):
        return jnp.where(
            core == 0, jnp.concatenate([mine, other], axis=1), jnp.concatenate([other, mine], axis=1)
        )

    def part_of(x, which):
        return jnp.concatenate([x[:, (2 * g + which) * HD : (2 * g + which + 1) * HD] for g in range(HEADS)], axis=1)

    k_grad = placed(part_of(dkv_mine, 0), part_of(dkv_far, 0))
    v_grad = placed(part_of(dkv_mine, 1), part_of(dkv_far, 1))
    q_grad = placed(dq_mine, dq_back)
    return q_grad, k_grad, v_grad, gain_grad


def solution(mesh):
    return jax.shard_map(
        local,
        mesh=mesh,
        in_specs=(
            P(("dp", "tensor"), None),
            P(("dp", "tensor"), None),
            P(("dp", "tensor"), None),
            P(),
            P(),
            P(("dp", "tensor"), None),
            P("dp", None),
            P(("dp", "tensor")),
        ),
        out_specs=(
            P(("dp", "tensor"), None),
            P(("dp", "tensor"), None),
            P(("dp", "tensor"), None),
            P(),
        ),
        check_vma=False,
    )
```

time: 146 us -> 130 us (0.89); the launches traced: 143 us -> 130 us
  starting transfers between devices: 81 us -> 60.6 us
  waiting for transfers between devices: 10.1 us -> 23.8 us
  Pallas kernels: 34.9 us -> 27.9 us
    ppermute x20 -> x9, starting transfers between devices: 39.2 us -> 19.4 us  [the longest x3 7.11 us: later(): lax.ppermute(x, 'tensor', [(t, t + 2 * n) for t in range(size - 2 * n)])]
    all_to_all x2, waiting for transfers between devices: 6.09 us -> 15.2 us  [gathered_sum(): return jnp.sum(lax.all_to_all(spread, axis, 0, 0, tiled=True), axis=0)]
    pallas_call x2 -> x1, Pallas kernels: 34.9 us -> 27.9 us  [attend(): pl.pallas_call(attend_kernel, grid_spec=pltpu.PrefetchScalarGridSpec(num_...]
    all_to_all x2, starting transfers between devices: 30.6 us -> 26.9 us  [gathered_sum(): return jnp.sum(lax.all_to_all(spread, axis, 0, 0, tiled=True), axis=0)]
    ppermute x20 -> x9, waiting for transfers between devices: 3.96 us -> 7.65 us  [the longest x3 7.64 us: later(): lax.ppermute(x, 'tensor', [(t, t + 2 * n) for t in range(size - 2 * n)])]
    ppermute x1, starting transfers between devices: 2.4 us -> 5.56 us  [local(): lax.ppermute(lax.dynamic_slice_in_dim(dkv, (1 - core) * ROWS, ROWS, 0), '...]
    another operation x3 -> x1, other arithmetic: 2.09 us -> 0.18 us
  transfers between devices with their start and end apart: 24 -> 13, of which waited for: 2 -> 4; matrix products, arithmetic and copies ran while one was open for 9% -> 10% of each run, Pallas kernels for 24% -> 0%
where the time goes in v2:
time: 130 us
  starting transfers between devices  60.6 us (47%)
  Pallas kernels  27.9 us (21%)
  waiting for transfers between devices  23.8 us (18%)
  other arithmetic  12.4 us (10%)
  local copies, waits for them, and re-layouts  3.93 us (3%)
    pallas_call x1, Pallas kernels, attend(): pl.pallas_call(attend_kernel, grid_spec=pltpu.PrefetchScalarGridSpec(num_...  27.9 us
    all_to_all x2, starting transfers between devices, gathered_sum(): return jnp.sum(lax.all_to_all(spread, axis, 0, 0, tiled=True), axis=0)  26.9 us
    all_to_all x2, waiting for transfers between devices, gathered_sum(): return jnp.sum(lax.all_to_all(spread, axis, 0, 0, tiled=True), axis=0)  15.2 us
    ppermute x1, starting transfers between devices, local(): kv_other = lax.ppermute(half(1 - core), 'tensor', swap)  8.79 us
    ppermute x3, waiting for transfers between devices, later(): lax.ppermute(x, 'tensor', [(t, t + 2 * n) for t in range(size - 2 * n)])  7.64 us
    ppermute x3, starting transfers between devices, later(): lax.ppermute(x, 'tensor', [(t, t + 2 * n) for t in range(size - 2 * n)])  7.11 us
    ppermute x1, starting transfers between devices, local(): lax.ppermute(lax.dynamic_slice_in_dim(dkv, (1 - core) * ROWS, ROWS, 0), '...  5.56 us
    ppermute x4, starting transfers between devices, earlier(): lax.ppermute(x, 'tensor', [(t + 2 * n, t) for t in range(size - 2 * n)])  5.17 us
  transfers between devices with their start and end apart: 13, of which 4 were waited for; matrix products, arithmetic and copies ran while one was open for 10% of the time, Pallas kernels for 0%

profile of v2, /device:TPU:1, one launch (start us, length us, event | category | flops | bytes accessed | tf_op | source)
XLA Modules:
  0.0 129.6 jit_solution(14633951528991096410)
XLA Ops:
  0.7 1.0 constant_dynamic-slice_fusion.10
  1.7 8.8 %collective-permute-start = (bf16[128,512]{1,0:T(8,128)(2,1)S(1)}, bf16[128,512]{1,0:T(8,128)(2,1)S(1)}, u32[]{:S(2)}, u32[]{:S(2)}) collective-permute-start(bf16[128,512]{1,0:T(8,128)(2,1)S(1)} %pad_maximum_fusion.6), channel_id=1, source_target_pairs={{0,1},{1,0},{2,3},{3,2},{4,5},{5,4},{6,7},{7,6},{8,9},{9,8},{10,11... | collective-permute-start | bytes 393224 | tf_op jit(solution)/shard_map/ppermute | solution.py:276
  10.6 0.9 collective-permute-done
  11.6 1.4 %collective-permute-start.2 = (bf16[256,512]{1,0:T(8,128)(2,1)S(1)}, bf16[256,512]{1,0:T(8,128)(2,1)S(1)}, u32[]{:S(2)}, u32[]{:S(2)}) collective-permute-start(bf16[256,512]{1,0:T(8,128)(2,1)S(1)} %pad_maximum_fusion.4.kv0), channel_id=1, source_target_pairs={{0,4},{1,5},{2,6},{3,7},{4,8},{5,9},{6,10},{7,11},{8,12},{9,13},{1... | collective-permute-start | bytes 786440 | tf_op jit(solution)/shard_map/ppermute | solution.py:281
  13.0 1.3 %collective-permute-start.3 = (bf16[256,512]{1,0:T(8,128)(2,1)S(1)}, bf16[256,512]{1,0:T(8,128)(2,1)S(1)}, u32[]{:S(2)}, u32[]{:S(2)}) collective-permute-start(bf16[256,512]{1,0:T(8,128)(2,1)S(1)} %pad_maximum_fusion.4.kv0), channel_id=1, source_target_pairs={{0,2},{1,3},{2,4},{3,5},{4,6},{5,7},{6,8},{7,9},{8,10},{9,11},{10,... | collective-permute-start | bytes 786440 | tf_op jit(solution)/shard_map/ppermute | solution.py:281
  15.1 2.8 %collective-permute-start.1 = (bf16[128,4096]{1,0:T(8,128)(2,1)S(1)}, bf16[128,4096]{1,0:T(8,128)(2,1)}, u32[]{:S(2)}, u32[]{:S(2)}) collective-permute-start(bf16[128,4096]{1,0:T(8,128)(2,1)S(1)} %pad_maximum_fusion), channel_id=1, source_target_pairs={{0,1},{1,0},{2,3},{3,2},{4,5},{5,4},{6,7},{7,6},{8,9},{9,8},{10,11... | collective-permute-start | bytes 3145736 | tf_op jit(solution)/shard_map/ppermute | solution.py:304
  18.2 2.4 %fusion = (f32[1280,64]{1,0:T(8,128)S(1)}, f32[1280,64]{1,0:T(8,128)S(1)}, f32[1280,64]{1,0:T(8,128)S(1)}) fusion(f32[64]{0:T(128)S(1)} %multiply_power_fusion, f32[1280]{0:T(1024)S(1)} %subtract_convert_fusion), kind=kLoop, calls=%fused_computation.13 | loop fusion | flops 163840 | bytes 988416 | tf_op jit(solution)/shard_map/neg | solution.py:291
  20.6 1.1 pad_maximum_fusion.1.cos
  21.6 1.1 pad_maximum_fusion.2.sin
  22.8 4.4 %collective-permute-start.4 = (bf16[512,512]{1,0:T(8,128)(2,1)S(1)}, bf16[512,512]{1,0:T(8,128)(2,1)S(1)}, u32[]{:S(2)}, u32[]{:S(2)}) collective-permute-start(bf16[512,512]{1,0:T(8,128)(2,1)S(1)} %pad_maximum_fusion.3), channel_id=1, source_target_pairs={{0,4},{1,5},{2,6},{3,7},{4,8},{5,9},{6,10},{7,11},{8,12},{9,13},{1... | collective-permute-start | bytes 1572872 | tf_op jit(solution)/shard_map/ppermute | solution.py:281
  27.2 0.6 slice_convert_fusion.qaug
  27.8 0.7 copy.14.wt
  28.6 1.0 select_convert_fusion.kaug
  29.5 7.6 %collective-permute-done.4.kv_far = bf16[512,512]{1,0:T(8,128)(2,1)S(1)} collective-permute-done((bf16[512,512]{1,0:T(8,128)(2,1)S(1)}, bf16[512,512]{1,0:T(8,128)(2,1)S(1)}, u32[]{:S(2)}, u32[]{:S(2)}) %collective-permute-start.4) | collective-permute-done | bytes 524320 | tf_op jit(solution)/shard_map/ppermute | solution.py:281
  37.2 0.8 copy-done.8
  38.0 27.9 %attend_back.1 = (bf16[128,2048]{1,0:T(8,128)(2,1)}, bf16[128,2048]{1,0:T(8,128)(2,1)}, bf16[256,512]{1,0:T(8,128)(2,1)}, bf16[256,512]{1,0:T(8,128)(2,1)}, bf16...) custom-call(s32[1]{0:T(128)} %bitcast.core_ref, ...), custom_call_target="tpu_custom_call" | custom-call | flops 6039797760 | bytes 4194304 | tf_op jit(solution)/shard_map/attend_back/pallas_call | solution.py:211
  65.9 1.3 collective-permute-start.6
  67.2 1.3 collective-permute-start.7
  68.5 1.3 collective-permute-start.8
  69.8 1.3 collective-permute-start.9
  71.1 0.7 bitcast_reduce_fusion
  71.8 0.6 broadcast_in_dim.75
  72.4 15.3 %all-to-all-start = ((f32[32,1,256]{2,1,0:T(1,128)}), f32[32,1,256]{2,1,0:T(1,128)S(1)}, u32[]{:S(2)}, u32[]{:S(2)}) async-start(f32[32,1,256]{2,1,0:T(1,128)} %broadcast_in_dim.75), calls=%async_computation | async-start | bytes 65536 | tf_op jit(solution)/shard_map/all_to_all | solution.py:317
  87.7 4.3 %collective-permute-start.5 = (bf16[128,2048]{1,0:T(8,128)(2,1)}, bf16[128,2048]{1,0:T(8,128)(2,1)S(1)}, u32[]{:S(2)}, u32[]{:S(2)}) collective-permute-start(bf16[128,2048]{1,0:T(8,128)(2,1)} %get-tuple-element.26), channel_id=1, source_target_pairs={{0,1},{1,0},{2,3},{3,2},{4,5},{5,4},{6,7},{7,6},{8,9},{9,8},{10,11... | collective-permute-start | bytes 1572872 | tf_op jit(solution)/shard_map/ppermute | solution.py:319
  92.1 7.9 %all-to-all-done = f32[32,1,256]{2,1,0:T(1,128)S(1)} async-done(((f32[32,1,256]{2,1,0:T(1,128)}), f32[32,1,256]{2,1,0:T(1,128)S(1)}, u32[]{:S(2)}, u32[]{:S(2)}) %all-to-all-start) | async-done | bytes 32800 | tf_op jit(solution)/shard_map/all_to_all | solution.py:317
  100.1 1.2 add_convert_fusion
  101.4 5.6 %collective-permute-start.10 = (bf16[128,512]{1,0:T(8,128)(2,1)S(1)}, bf16[128,512]{1,0:T(8,128)(2,1)S(1)}, u32[]{:S(2)}, u32[]{:S(2)}) collective-permute-start(bf16[128,512]{1,0:T(8,128)(2,1)S(1)} %constant_dynamic-slice_fusion.1), channel_id=1, source_target_pairs={{0,1},{1,0},{2,3},{3,2},{4,5},{5,4},{6,7},{7,6},{8,9},{9,8},{10,11... | collective-permute-start | bytes 393224 | tf_op jit(solution)/shard_map/ppermute | solution.py:331
  107.5 11.6 %all-to-all-start.1 = ((f32[16,1,256]{2,1,0:T(1,128)}), f32[16,1,256]{2,1,0:T(1,128)S(1)}, u32[]{:S(2)}, u32[]{:S(2)}) async-start(f32[16,1,256]{2,1,0:T(1,128)} %broadcast_in_dim.77), calls=%async_computation.1 | async-start | bytes 32768 | tf_op jit(solution)/shard_map/all_to_all | solution.py:317
  119.1 7.3 %all-to-all-done.1 = f32[16,1,256]{2,1,0:T(1,128)S(1)} async-done(((f32[16,1,256]{2,1,0:T(1,128)}), f32[16,1,256]{2,1,0:T(1,128)S(1)}, u32[]{:S(2)}, u32[]{:S(2)}) %all-to-all-start.1) | async-done | bytes 16416 | tf_op jit(solution)/shard_map/all_to_all | solution.py:317
  127.0 0.7 maximum_select_fusion.2
  127.7 0.7 maximum_select_fusion.1
  128.4 1.2 maximum_select_fusion
  (50 shorter events, 2.5 us)
Async XLA Ops:
  0.6 13.7 %copy-start.6 = (s32[1,4]{1,0:T(1,128)S(1)}, s32[1,4]{1,0:T(1,128)}, u32[]{:S(2)}) copy-start(s32[1,4]{1,0:T(1,128)} %param.14) | copy-start | bytes 52
  0.6 14.1 %copy-start.1 = (bf16[128,4096]{1,0:T(8,128)(2,1)S(1)}, bf16[128,4096]{1,0:T(8,128)(2,1)}, u32[]{:S(2)}) copy-start(bf16[128,4096]{1,0:T(8,128)(2,1)} %q_own) | copy-start | bytes 3145732
  1.7 9.8 %collective-permute-start = (bf16[128,512]{1,0:T(8,128)(2,1)S(1)}, bf16[128,512]{1,0:T(8,128)(2,1)S(1)}, u32[]{:S(2)}, u32[]{:S(2)}) collective-permute-start(bf16[128,512]{1,0:T(8,128)(2,1)S(1)} %pad_maximum_fusion.6), channel_id=1, source_target_pairs={{0,1},{1,0},{2,3},{3,2},{4,5},{5,4},{6,7},{7,6},{8,9},{9,8},{10,11... | collective-permute-start | bytes 393224 | tf_op jit(solution)/shard_map/ppermute | solution.py:276
  11.5 3.3 %copy-start.7 = (s32[128]{0:T(128)S(1)}, s32[128]{0:T(128)}, u32[]{:S(2)}) copy-start(s32[128]{0:T(128)} %param.15) | copy-start | bytes 1540
  11.5 3.4 %copy-start.2 = (bf16[128,4096]{1,0:T(8,128)(2,1)S(1)}, bf16[128,4096]{1,0:T(8,128)(2,1)}, u32[]{:S(2)}) copy-start(bf16[128,4096]{1,0:T(8,128)(2,1)} %g_own) | copy-start | bytes 3145732
  11.6 3.5 %copy-start.3 = (bf16[256,512]{1,0:T(8,128)(2,1)}, bf16[256,512]{1,0:T(8,128)(2,1)S(1)}, u32[]{:S(2)}) copy-start(bf16[256,512]{1,0:T(8,128)(2,1)S(1)} %pad_maximum_fusion.4.kv0) | copy-start | bytes 786436
  11.6 11.2 %collective-permute-start.2 = (bf16[256,512]{1,0:T(8,128)(2,1)S(1)}, bf16[256,512]{1,0:T(8,128)(2,1)S(1)}, u32[]{:S(2)}, u32[]{:S(2)}) collective-permute-start(bf16[256,512]{1,0:T(8,128)(2,1)S(1)} %pad_maximum_fusion.4.kv0), channel_id=1, source_target_pairs={{0,4},{1,5},{2,6},{3,7},{4,8},{5,9},{6,10},{7,11},{8,12},{9,13},{1... | collective-permute-start | bytes 786440 | tf_op jit(solution)/shard_map/ppermute | solution.py:281
  13.0 9.8 %collective-permute-start.3 = (bf16[256,512]{1,0:T(8,128)(2,1)S(1)}, bf16[256,512]{1,0:T(8,128)(2,1)S(1)}, u32[]{:S(2)}, u32[]{:S(2)}) collective-permute-start(bf16[256,512]{1,0:T(8,128)(2,1)S(1)} %pad_maximum_fusion.4.kv0), channel_id=1, source_target_pairs={{0,2},{1,3},{2,4},{3,5},{4,6},{5,7},{6,8},{7,9},{8,10},{9,11},{10,... | collective-permute-start | bytes 786440 | tf_op jit(solution)/shard_map/ppermute | solution.py:281
  15.1 22.0 %collective-permute-start.1 = (bf16[128,4096]{1,0:T(8,128)(2,1)S(1)}, bf16[128,4096]{1,0:T(8,128)(2,1)}, u32[]{:S(2)}, u32[]{:S(2)}) collective-permute-start(bf16[128,4096]{1,0:T(8,128)(2,1)S(1)} %pad_maximum_fusion), channel_id=1, source_target_pairs={{0,1},{1,0},{2,3},{3,2},{4,5},{5,4},{6,7},{7,6},{8,9},{9,8},{10,11... | collective-permute-start | bytes 3145736 | tf_op jit(solution)/shard_map/ppermute | solution.py:304
  22.8 14.4 %copy-start.4 = (bf16[256,512]{1,0:T(8,128)(2,1)}, bf16[256,512]{1,0:T(8,128)(2,1)S(1)}, u32[]{:S(2)}) copy-start(bf16[256,512]{1,0:T(8,128)(2,1)S(1)} %collective-permute-done.2.kv2) | copy-start | bytes 786436
  22.8 14.4 %copy-start.5 = (bf16[256,512]{1,0:T(8,128)(2,1)}, bf16[256,512]{1,0:T(8,128)(2,1)S(1)}, u32[]{:S(2)}) copy-start(bf16[256,512]{1,0:T(8,128)(2,1)S(1)} %collective-permute-done.3.kv1) | copy-start | bytes 786436
  22.8 14.3 %collective-permute-start.4 = (bf16[512,512]{1,0:T(8,128)(2,1)S(1)}, bf16[512,512]{1,0:T(8,128)(2,1)S(1)}, u32[]{:S(2)}, u32[]{:S(2)}) collective-permute-start(bf16[512,512]{1,0:T(8,128)(2,1)S(1)} %pad_maximum_fusion.3), channel_id=1, source_target_pairs={{0,4},{1,5},{2,6},{3,7},{4,8},{5,9},{6,10},{7,11},{8,12},{9,13},{1... | collective-permute-start | bytes 1572872 | tf_op jit(solution)/shard_map/ppermute | solution.py:281
  37.2 0.8 copy-start.8
  65.9 34.2 %collective-permute-start.6 = (bf16[256,512]{1,0:T(8,128)(2,1)}, bf16[256,512]{1,0:T(8,128)(2,1)S(1)}, u32[]{:S(2)}, u32[]{:S(2)}) collective-permute-start(bf16[256,512]{1,0:T(8,128)(2,1)} %get-tuple-element.29), channel_id=1, source_target_pairs={{8,0},{9,1},{10,2},{11,3},{12,4},{13,5},{14,6},{15,7},{24,16},{25,... | collective-permute-start | bytes 786440 | tf_op jit(solution)/shard_map/ppermute | solution.py:322
  67.2 32.9 %collective-permute-start.7 = (bf16[256,512]{1,0:T(8,128)(2,1)}, bf16[256,512]{1,0:T(8,128)(2,1)S(1)}, u32[]{:S(2)}, u32[]{:S(2)}) collective-permute-start(bf16[256,512]{1,0:T(8,128)(2,1)} %get-tuple-element.30), channel_id=1, source_target_pairs={{6,0},{7,1},{8,2},{9,3},{10,4},{11,5},{12,6},{13,7},{14,8},{15,9},... | collective-permute-start | bytes 786440 | tf_op jit(solution)/shard_map/ppermute | solution.py:322
  68.5 31.6 %collective-permute-start.8 = (bf16[256,512]{1,0:T(8,128)(2,1)}, bf16[256,512]{1,0:T(8,128)(2,1)S(1)}, u32[]{:S(2)}, u32[]{:S(2)}) collective-permute-start(bf16[256,512]{1,0:T(8,128)(2,1)} %get-tuple-element.31), channel_id=1, source_target_pairs={{4,0},{5,1},{6,2},{7,3},{8,4},{9,5},{10,6},{11,7},{12,8},{13,9},{1... | collective-permute-start | bytes 786440 | tf_op jit(solution)/shard_map/ppermute | solution.py:322
  69.8 30.3 %collective-permute-start.9 = (bf16[256,512]{1,0:T(8,128)(2,1)}, bf16[256,512]{1,0:T(8,128)(2,1)S(1)}, u32[]{:S(2)}, u32[]{:S(2)}) collective-permute-start(bf16[256,512]{1,0:T(8,128)(2,1)} %get-tuple-element.32), channel_id=1, source_target_pairs={{2,0},{3,1},{4,2},{5,3},{6,4},{7,5},{8,6},{9,7},{10,8},{11,9},{12,... | collective-permute-start | bytes 786440 | tf_op jit(solution)/shard_map/ppermute | solution.py:322
  72.4 27.6 %all-to-all-start = ((f32[32,1,256]{2,1,0:T(1,128)}), f32[32,1,256]{2,1,0:T(1,128)S(1)}, u32[]{:S(2)}, u32[]{:S(2)}) async-start(f32[32,1,256]{2,1,0:T(1,128)} %broadcast_in_dim.75), calls=%async_computation | async-start | bytes 65536 | tf_op jit(solution)/shard_map/all_to_all | solution.py:317
  87.7 40.7 %collective-permute-start.5 = (bf16[128,2048]{1,0:T(8,128)(2,1)}, bf16[128,2048]{1,0:T(8,128)(2,1)S(1)}, u32[]{:S(2)}, u32[]{:S(2)}) collective-permute-start(bf16[128,2048]{1,0:T(8,128)(2,1)} %get-tuple-element.26), channel_id=1, source_target_pairs={{0,1},{1,0},{2,3},{3,2},{4,5},{5,4},{6,7},{7,6},{8,9},{9,8},{10,11... | collective-permute-start | bytes 1572872 | tf_op jit(solution)/shard_map/ppermute | solution.py:319
  101.3 27.1 %copy-start = (bf16[128,2048]{1,0:T(8,128)(2,1)S(1)}, bf16[128,2048]{1,0:T(8,128)(2,1)}, u32[]{:S(2)}) copy-start(bf16[128,2048]{1,0:T(8,128)(2,1)} %get-tuple-element.25) | copy-start | bytes 1572868
  101.4 25.7 %collective-permute-start.10 = (bf16[128,512]{1,0:T(8,128)(2,1)S(1)}, bf16[128,512]{1,0:T(8,128)(2,1)S(1)}, u32[]{:S(2)}, u32[]{:S(2)}) collective-permute-start(bf16[128,512]{1,0:T(8,128)(2,1)S(1)} %constant_dynamic-slice_fusion.1), channel_id=1, source_target_pairs={{0,1},{1,0},{2,3},{3,2},{4,5},{5,4},{6,7},{7,6},{8,9},{9,8},{10,11... | collective-permute-start | bytes 393224 | tf_op jit(solution)/shard_map/ppermute | solution.py:331
  107.5 18.9 %all-to-all-start.1 = ((f32[16,1,256]{2,1,0:T(1,128)}), f32[16,1,256]{2,1,0:T(1,128)S(1)}, u32[]{:S(2)}, u32[]{:S(2)}) async-start(f32[16,1,256]{2,1,0:T(1,128)} %broadcast_in_dim.77), calls=%async_computation.1 | async-start | bytes 32768 | tf_op jit(solution)/shard_map/all_to_all | solution.py:317

commit v3 on v2

--- a/solution.py
+++ b/solution.py
@@ -48,9 +48,9 @@
 
 
 def attend_kernel(
-    core_ref, q_own, g_own, rq, kv_far, kv2, kv1, kv0, cos, sin, kaug, qaug, wt, qgain, kgain,
+    core_ref, qt, gt, q_own, q_far, kv_far, kv2, kv1, kv0, cos, sin, kaug, qgain, kgain,
     dq_own, dq_far, dkv4, dkv3, dkv2, dkv1, dkv0, gains,
-    kt, vt, qt, gt, s_buf, dp_buf, p_scr, ds_scr, dk_acc, dv_acc,
+    kt, vt, s_buf, dp_buf, p_scr, ds_scr, dk_acc, dv_acc,
 ):
     core = core_ref[0]
     blocks = (kv_far.at[:CHIP], kv_far.at[CHIP:], kv2, kv1, kv0)
@@ -63,25 +63,7 @@
         kt[rows, :HD] = turn(unit * kg, cos[rows, :], sin[rows, :]).astype(bf16)
         kt[rows, HD:] = kaug[rows, :]
         vt[rows, :] = blk[:, HD:]
-    offs = []
-    for j in range(2):
-        b = core if j == 0 else 1 - core
-        off = pl.multiple_of(b * ROWS, ROWS)
-        offs.append(off)
-        c = cos[pl.ds(BACK * CHIP + off, ROWS), :]
-        s = sin[pl.ds(BACK * CHIP + off, ROWS), :]
-        hot = qaug[pl.ds(off, ROWS), :]
-        for h in range(GROUP):
-            cols = slice(h * HD, (h + 1) * HD)
-            rows = slice(h * ROWS, (h + 1) * ROWS)
-            raw = q_own[:, cols] if j == 0 else rq[:, cols]
-            unit, _ = unit_of(raw)
-            qt[j, rows, :HD] = turn(unit * qg, c, s).astype(bf16)
-            qt[j, rows, HD:] = hot
-            if j == 0:
-                gt[j, rows, :] = (g_own[:, cols].astype(f32) * wt[...]).astype(bf16)
-            else:
-                gt[j, rows, :] = rq[:, GROUP * HD + h * HD : GROUP * HD + (h + 1) * HD]
+    offs = [pl.multiple_of(b * ROWS, ROWS) for b in (core, 1 - core)]
 
     dk_acc[...] = jnp.zeros_like(dk_acc)
     dv_acc[...] = jnp.zeros_like(dv_acc)
@@ -113,14 +95,14 @@
     def scores(n, c):
         j = tiles[n][0]
         here = slice(c * PART, (c + 1) * PART)
-        s = lax.dot_general(kt[keys_of(n, c), :], qt[j, cols_of(n), :], nt, preferred_element_type=f32)
+        s = lax.dot_general(kt[keys_of(n, c), :], qt[0, j, cols_of(n), :], nt, preferred_element_type=f32)
         if c == chunks - 1:
             s = jnp.concatenate([s[: PART - ROWS], jnp.where(causal, s[PART - ROWS :], far)], axis=0)
         s_buf[n % 3, here, :] = s
         top = fold(s, jnp.maximum)
         peaks[n] = jnp.maximum(peaks[n], top) if c else top
         dp_buf[n % 3, here, :] = lax.dot_general(
-            vt[keys_of(n, c), :], gt[j, cols_of(n), :], nt, preferred_element_type=f32
+            vt[keys_of(n, c), :], gt[0, j, cols_of(n), :], nt, preferred_element_type=f32
         )
 
     def weights(n, c):
@@ -152,7 +134,7 @@
         for u in range(2):
             h = hp * 2 + u
             cols = slice(h * HD, (h + 1) * HD)
-            raw = q_own[:, cols] if j == 0 else rq[:, cols]
+            raw = q_own[:, cols] if j == 0 else q_far[:, cols]
             unit, inv = unit_of(raw)
             grad, part = norm_back(dq[u * ROWS : (u + 1) * ROWS, :], unit, inv, qg, c, s)
             gain_rows[0] = gain_rows[0] + part
@@ -166,8 +148,8 @@
         both = slice((hp - 1) * PAIR, (hp + 1) * PAIR)
         here = slice(c * PART, (c + 1) * PART)
         keys = keys_of(n, c)
-        dv_acc[keys, :] += lax.dot_general(p_scr[j, here, both], gt[j, both, :], nn, preferred_element_type=f32)
-        dk_acc[keys, :] += lax.dot_general(ds_scr[j, here, both], qt[j, both, :HD], nn, preferred_element_type=f32)
+        dv_acc[keys, :] += lax.dot_general(p_scr[j, here, both], gt[0, j, both, :], nn, preferred_element_type=f32)
+        dk_acc[keys, :] += lax.dot_general(ds_scr[j, here, both], qt[0, j, both, :HD], nn, preferred_element_type=f32)
 
     for step in range(total + 3):
         for c in range(chunks):
@@ -196,7 +178,53 @@
     gains[...] = rows + jnp.where(begun, gains[...], 0.0)
 
 
-def attend(core, q_states, out_grad, rq, kvs, cos, sin, kaug, qaug, wt, qgain, kgain):
+def query_kernel(core_ref, q_own, g_own, rq, cos, sin, qaug, wt, qgain, qt, gt):
+    core = core_ref[0]
+    gain = qgain[...]
+    for j in range(2):
+        at = pl.ds(pl.multiple_of((core if j == 0 else 1 - core) * ROWS, ROWS), ROWS)
+        c, s, hot = cos[at, :], sin[at, :], qaug[at, :]
+        for h in range(GROUP):
+            cols = slice(h * HD, (h + 1) * HD)
+            rows = slice(h * ROWS, (h + 1) * ROWS)
+            unit, _ = unit_of(q_own[:, cols] if j == 0 else rq[:, cols])
+            qt[0, j, rows, :HD] = turn(unit * gain, c, s).astype(bf16)
+            qt[0, j, rows, HD:] = hot
+            grad = g_own[:, cols] if j == 0 else rq[:, GROUP * HD + h * HD : GROUP * HD + (h + 1) * HD]
+            gt[0, j, rows, :] = (grad.astype(f32) * wt[:, j : j + 1]).astype(bf16)
+
+
+def queries(core, q_states, out_grad, rq, cos, sin, qaug, wt, qgain):
+    wide = GROUP * HD
+
+    def whole(shape, at=(0, 0)):
+        return pl.BlockSpec(shape, lambda g, c: at)
+
+    mine = pl.BlockSpec((ROWS, wide), lambda g, c: (0, 2 * c[0] + g))
+    own_rows = whole((CHIP, HD), (BACK, 0))
+    out = (HEADS, 2, GROUP * ROWS)
+    size = 1
+    for n in out:
+        size *= n
+    return pl.pallas_call(
+        query_kernel,
+        grid_spec=pltpu.PrefetchScalarGridSpec(
+            num_scalar_prefetch=1,
+            grid=(HEADS,),
+            in_specs=[mine, mine, pl.BlockSpec((ROWS, 2 * wide), lambda g, c: (0, g)), own_rows, own_rows]
+            + [whole((CHIP, HD)), whole((ROWS, 2)), whole((1, HD))],
+            out_specs=[
+                pl.BlockSpec((1, 2, GROUP * ROWS, n), lambda g, c: (g, 0, 0, 0)) for n in (2 * HD, HD)
+            ],
+        ),
+        out_shape=[jax.ShapeDtypeStruct(out + (n,), bf16) for n in (2 * HD, HD)],
+        compiler_params=pltpu.CompilerParams(vmem_limit_bytes=38 * 2**20),
+        cost_estimate=pl.CostEstimate(flops=40 * size * HD, bytes_accessed=5 * 2**20, transcendentals=size),
+        name="queries",
+    )(core, q_states, out_grad, rq, cos, sin, qaug, wt, qgain)
+
+
+def attend(core, qt, gt, q_states, rq, kvs, cos, sin, kaug, qgain, kgain):
     wide = GROUP * HD
 
     def whole(shape):
@@ -213,18 +241,19 @@
         grid_spec=pltpu.PrefetchScalarGridSpec(
             num_scalar_prefetch=1,
             grid=(HEADS,),
-            in_specs=[mine, mine, column((ROWS, 2 * wide))]
+            in_specs=[
+                pl.BlockSpec((1, 2, GROUP * ROWS, n), lambda g, c: (g, 0, 0, 0)) for n in (2 * HD, HD)
+            ]
+            + [mine, pl.BlockSpec((ROWS, wide), lambda g, c: (0, 2 * g))]
             + [column((2 * CHIP, 2 * HD))] + [column((CHIP, 2 * HD))] * 3
             + [whole((WIN, HD))] * 3
-            + [whole((CHIP, HD)), whole((ROWS, 1)), whole((1, HD)), whole((1, HD))],
+            + [whole((1, HD)), whole((1, HD))],
             out_specs=[column((ROWS, wide))] * 2
             + [column((CHIP, 2 * HD))] * (BACK + 1)
             + [whole((16, HD))],
             scratch_shapes=[
                 pltpu.VMEM((WIN, 2 * HD), bf16),
                 pltpu.VMEM((WIN, HD), bf16),
-                pltpu.VMEM((2, GROUP * ROWS, 2 * HD), bf16),
-                pltpu.VMEM((2, GROUP * ROWS, HD), bf16),
                 pltpu.VMEM((3, SPAN, PAIR), f32),
                 pltpu.VMEM((3, SPAN, PAIR), f32),
                 pltpu.VMEM((2, SPAN, GROUP * ROWS), bf16),
@@ -236,10 +265,10 @@
         out_shape=[sds((ROWS, HEADS * wide), bf16)] * 2
         + [sds((CHIP, HEADS * 2 * HD), bf16)] * BACK
         + [sds((CHIP, HEADS * 2 * HD), f32), sds((16, HD), f32)],
-        compiler_params=pltpu.CompilerParams(vmem_limit_bytes=58 * 2**20),
+        compiler_params=pltpu.CompilerParams(vmem_limit_bytes=38 * 2**20),
         cost_estimate=pl.CostEstimate(flops=pairs * HD * 2 * 5, bytes_accessed=4 * 2**20, transcendentals=pairs),
         name="attend_back",
-    )(core, q_states, out_grad, rq, *kvs, cos, sin, kaug, qaug, wt, qgain, kgain)
+    )(core, qt, gt, q_states, rq, *kvs, cos, sin, kaug, qgain, kgain)
 
 
 def window_layout(lens, first):
@@ -276,12 +305,20 @@
     kv_other = lax.ppermute(half(1 - core), "tensor", swap)
     first, second = (jnp.where(core == 0, a, b) for a, b in ((kv_mine, kv_other), (kv_other, kv_mine)))
     kv_chip = jnp.concatenate([first, second], axis=0)
-    kv_chip, lens, q_states, out_grad = lax.optimization_barrier((kv_chip, lengths[0], q_states, out_grad))
+    kv_chip, q_states, out_grad = lax.optimization_barrier((kv_chip, q_states, out_grad))
     def later(x, n):
         return lax.ppermute(x, "tensor", [(t, t + 2 * n) for t in range(size - 2 * n)])
 
     kv1, kv2 = later(kv_chip, 1), later(kv_chip, 2)
     kvs = [later(jnp.concatenate([kv2, kv1], axis=0), 2), kv2, kv1, kv_chip]
+
+    pieces = []
+    for g in range(HEADS):
+        head = HEADS * (1 - core) + g
+        pieces += [heads_of(q_states, head, wide), heads_of(out_grad, head, wide)]
+    pieces.append(jnp.broadcast_to(advantage.astype(bf16)[:, None], (ROWS, HD)))
+    rq = lax.ppermute(jnp.concatenate(pieces, axis=1), "tensor", swap)
+    lens = lax.optimization_barrier((lengths[0], kv2))[0]
 
     segment, position, length = window_layout(lens, chip * CHIP)
     frequency = rope_base ** (-jnp.arange(HD // 2, dtype=f32) * 2.0 / HD)
@@ -293,19 +330,15 @@
     same = segment[:, None] == lane
     kaug = jnp.where(same | (lane >= lengths.shape[1]), 0.0, far).astype(bf16)
     qaug = same[BACK * CHIP :].astype(bf16)
-    own_len = lax.dynamic_slice_in_dim(length, BACK * CHIP + core * ROWS, ROWS, 0)
-    weight = advantage.astype(f32) / 32.0 * (group_rows / lengths.shape[1]) / own_len.astype(f32)
-    wt = weight[:, None]
-
-    pieces = []
-    for g in range(HEADS):
-        head = HEADS * (1 - core) + g
-        pieces += [heads_of(q_states, head, wide), (heads_of(out_grad, head, wide).astype(f32) * wt).astype(bf16)]
-    rq = lax.ppermute(jnp.concatenate(pieces, axis=1), "tensor", swap)
-
-    outs = attend(
-        core.astype(jnp.int32)[None], q_states, out_grad, rq, kvs, cos, sin, kaug, qaug, wt, q_gain[None], k_gain[None]
-    )
+    wt = []
+    for who, adv in ((core, advantage), (1 - core, rq[:, 2 * HEADS * wide])):
+        resp = lax.dynamic_slice_in_dim(length, BACK * CHIP + who * ROWS, ROWS, 0)
+        wt.append(adv.astype(f32) / 32.0 * (group_rows / lengths.shape[1]) / resp.astype(f32))
+    wt = jnp.stack(wt, axis=1)
+
+    core_arr = core.astype(jnp.int32)[None]
+    qt, gt = queries(core_arr, q_states, out_grad, rq, cos, sin, qaug, wt, q_gain[None])
+    outs = attend(core_arr, qt, gt, q_states, rq, kvs, cos, sin, kaug, q_gain[None], k_gain[None])
     dq_mine, dq_far, *parts, dkv, gain_rows = outs
 
     gains = jnp.sum(gain_rows.reshape(2, 8, HD), axis=1)
@@ -323,7 +356,7 @@
 
     back = [earlier(part, n) for n, part in zip(range(BACK, 0, -1), parts)]
     gains, back = lax.optimization_barrier((gathered_sum(gains, "dp"), back))
-    gain_grad = gathered_sum(gains, "tensor").reshape(2, HD) / group_rows
+    gains = gathered_sum(gains, "tensor")
     for part in back:
         dkv = dkv + part.astype(f32)
     dkv = dkv.astype(bf16)
@@ -341,7 +374,7 @@
     k_grad = placed(part_of(dkv_mine, 0), part_of(dkv_far, 0))
     v_grad = placed(part_of(dkv_mine, 1), part_of(dkv_far, 1))
     q_grad = placed(dq_mine, dq_back)
-    return q_grad, k_grad, v_grad, gain_grad
+    return q_grad, k_grad, v_grad, gains.reshape(2, HD) / group_rows
 
 
 def solution(mesh):

time: 130 us -> 128 us (0.985)
  waiting for transfers between devices: 23.8 us -> 16.1 us
  local copies, waits for them, and re-layouts: 3.93 us -> 7 us
  Pallas kernels: 27.9 us -> 30.8 us
  other arithmetic: 12.4 us -> 10.5 us
    ppermute x3, waiting for transfers between devices: 7.64 us -> 0.01 us  [later(): lax.ppermute(x, 'tensor', [(t, t + 2 * n) for t in range(size - 2 * n)])]
    pallas_call x0 -> x1, Pallas kernels: none -> 5.37 us  [queries(): pl.pallas_call(query_kernel, grid_spec=pltpu.PrefetchScalarGridSpec(num_s...]
    unnamed x18 -> x32, local copies, waits for them, and re-layouts: 0.85 us -> 3.89 us
    pallas_call x1, Pallas kernels: 27.9 us -> 25.4 us  [attend(): pl.pallas_call(attend_kernel, grid_spec=pltpu.PrefetchScalarGridSpec(num_...]
    ppermute x3, starting transfers between devices: 7.11 us -> 9.15 us  [later(): lax.ppermute(x, 'tensor', [(t, t + 2 * n) for t in range(size - 2 * n)])]
  transfers between devices with their start and end apart: 13 -> 13, of which waited for: 4 -> 3; matrix products, arithmetic and copies ran while one was open for 10% -> 11% of each run, Pallas kernels for 0% -> 4%
where the time goes in v3:
time: 128 us; the launch traced here: 127 us
  starting transfers between devices  61.4 us (48%)
  Pallas kernels  30.8 us (24%)
  waiting for transfers between devices  16.1 us (13%)
  other arithmetic  10.5 us (8%)
  local copies, waits for them, and re-layouts  7 us (5%)
    all_to_all x2, starting transfers between devices, gathered_sum(): return jnp.sum(lax.all_to_all(spread, axis, 0, 0, tiled=True), axis=0)  26.9 us
    pallas_call x1, Pallas kernels, attend(): pl.pallas_call(attend_kernel, grid_spec=pltpu.PrefetchScalarGridSpec(num_...  25.4 us
    all_to_all x2, waiting for transfers between devices, gathered_sum(): return jnp.sum(lax.all_to_all(spread, axis, 0, 0, tiled=True), axis=0)  15.8 us
    ppermute x3, starting transfers between devices, later(): lax.ppermute(x, 'tensor', [(t, t + 2 * n) for t in range(size - 2 * n)])  9.15 us
    ppermute x1, starting transfers between devices, local(): kv_other = lax.ppermute(half(1 - core), 'tensor', swap)  8.92 us
    pallas_call x1, Pallas kernels, queries(): pl.pallas_call(query_kernel, grid_spec=pltpu.PrefetchScalarGridSpec(num_s...  5.37 us
    ppermute x4, starting transfers between devices, earlier(): lax.ppermute(x, 'tensor', [(t + 2 * n, t) for t in range(size - 2 * n)])  5.16 us
    ppermute x1, starting transfers between devices, local(): lax.ppermute(lax.dynamic_slice_in_dim(dkv, (1 - core) * ROWS, ROWS, 0), '...  4.85 us
  transfers between devices with their start and end apart: 13, of which 3 were waited for; matrix products, arithmetic and copies ran while one was open for 11% of the time, Pallas kernels for 4%

profile of v3, /device:TPU:1, one launch (start us, length us, event | category | flops | bytes accessed | tf_op | source)
XLA Modules:
  0.0 127.0 jit_solution(14060301574632340640)
XLA Ops:
  0.7 1.0 constant_dynamic-slice_fusion.8
  1.7 8.9 %collective-permute-start = (bf16[128,512]{1,0:T(8,128)(2,1)S(1)}, bf16[128,512]{1,0:T(8,128)(2,1)S(1)}, u32[]{:S(2)}, u32[]{:S(2)}) collective-permute-start(bf16[128,512]{1,0:T(8,128)(2,1)S(1)} %pad_maximum_fusion.5), channel_id=1, source_target_pairs={{0,1},{1,0},{2,3},{3,2},{4,5},{5,4},{6,7},{7,6},{8,9},{9,8},{10,11... | collective-permute-start | bytes 393224 | tf_op jit(solution)/shard_map/ppermute | solution.py:305
  10.7 0.7 convert_element_type.47
  11.7 1.4 %collective-permute-start.2 = (bf16[256,512]{1,0:T(8,128)(2,1)S(1)}, bf16[256,512]{1,0:T(8,128)(2,1)S(1)}, u32[]{:S(2)}, u32[]{:S(2)}) collective-permute-start(bf16[256,512]{1,0:T(8,128)(2,1)S(1)} %pad_maximum_fusion.3.kv0), channel_id=1, source_target_pairs={{0,4},{1,5},{2,6},{3,7},{4,8},{5,9},{6,10},{7,11},{8,12},{9,13},{1... | collective-permute-start | bytes 786440 | tf_op jit(solution)/shard_map/ppermute | solution.py:310
  13.1 1.3 %collective-permute-start.3 = (bf16[256,512]{1,0:T(8,128)(2,1)S(1)}, bf16[256,512]{1,0:T(8,128)(2,1)S(1)}, u32[]{:S(2)}, u32[]{:S(2)}) collective-permute-start(bf16[256,512]{1,0:T(8,128)(2,1)S(1)} %pad_maximum_fusion.3.kv0), channel_id=1, source_target_pairs={{0,2},{1,3},{2,4},{3,5},{4,6},{5,7},{6,8},{7,9},{8,10},{9,11},{10,... | collective-permute-start | bytes 786440 | tf_op jit(solution)/shard_map/ppermute | solution.py:310
  14.5 0.8 dynamic-slice_dynamic-update-slice_fusion.3
  15.2 0.8 dynamic-slice_dynamic-update-slice_fusion.2
  16.0 0.8 dynamic-slice_dynamic-update-slice_fusion.1
  16.8 0.7 dynamic-slice_dynamic-update-slice_fusion
  17.5 0.7 broadcast_dynamic-update-slice_fusion
  18.2 2.8 %collective-permute-start.1 = (bf16[128,4224]{1,0:T(8,128)(2,1)}, bf16[128,4224]{1,0:T(8,128)(2,1)}, u32[]{:S(2)}, u32[]{:S(2)}) collective-permute-start(bf16[128,4224]{1,0:T(8,128)(2,1)} %broadcast_dynamic-update-slice_fusion), channel_id=1, source_target_pairs={{0,1},{1,0},{2,3},{3,2},{4,5},{5,4},{6,7},{7,6},{8,9},{9,8},{10,11... | collective-permute-start | bytes 3244040 | tf_op jit(solution)/shard_map/ppermute | solution.py:320
  21.6 0.9 pad_maximum_fusion.2
  22.5 6.4 %collective-permute-start.4 = (bf16[512,512]{1,0:T(8,128)(2,1)}, bf16[512,512]{1,0:T(8,128)(2,1)}, u32[]{:S(2)}, u32[]{:S(2)}) collective-permute-start(bf16[512,512]{1,0:T(8,128)(2,1)} %pad_maximum_fusion.2), channel_id=1, source_target_pairs={{0,4},{1,5},{2,6},{3,7},{4,8},{5,9},{6,10},{7,11},{8,12},{9,13},{1... | collective-permute-start | bytes 1572872 | tf_op jit(solution)/shard_map/ppermute | solution.py:310
  28.9 2.4 %fusion = (f32[1280,64]{1,0:T(8,128)S(1)}, f32[1280,64]{1,0:T(8,128)S(1)}, f32[1280,64]{1,0:T(8,128)S(1)}) fusion(f32[64]{0:T(128)S(1)} %multiply_power_fusion, f32[1280]{0:T(1024)S(1)} %subtract_convert_fusion), kind=kLoop, calls=%fused_computation.14 | loop fusion | flops 163840 | bytes 988416 | tf_op jit(solution)/shard_map/neg | solution.py:328
  31.8 1.0 select_convert_fusion.kaug
  32.9 0.9 multiply_reduce_fusion
  34.0 5.4 %queries.1 = (bf16[2,2,1024,256]{3,2,1,0:T(8,128)(2,1)S(1)}, bf16[2,2,1024,128]{3,2,1,0:T(8,128)(2,1)S(1)}) custom-call(s32[1]{0:T(128)} %bitcast.core_ref, bf16[128,4096]{1,0:T(8,128)(2,1)S(1)} %copy-done.1, bf16[128,4096]{1,0:T(8,128)(2,1)S(1)} %copy-done, bf16[128,4224]{1,0:T(8,128)(2,1)} %collective-permute-done.1.rq.q_far, ...), custom_call_target="tpu_custom_call" | custom-call | flops 20971520 | bytes 5242880 | tf_op jit(solution)/shard_map/queries/pallas_call | solution.py:209
  39.5 25.4 %attend_back.1 = (bf16[128,2048]{1,0:T(8,128)(2,1)S(1)}, bf16[128,2048]{1,0:T(8,128)(2,1)S(1)}, bf16[256,512]{1,0:T(8,128)(2,1)}, bf16[256,512]{1,0:T(8,128)(2,1...) custom-call(s32[1]{0:T(128)} %bitcast.core_ref, ...), custom_call_target="tpu_custom_call" | custom-call | flops 6039797760 | bytes 4194304 | tf_op jit(solution)/shard_map/attend_back/pallas_call | solution.py:239
  64.9 0.8 copy-done.10
  65.7 1.3 %collective-permute-start.6 = (bf16[256,512]{1,0:T(8,128)(2,1)}, bf16[256,512]{1,0:T(8,128)(2,1)S(1)}, u32[]{:S(2)}, u32[]{:S(2)}) collective-permute-start(bf16[256,512]{1,0:T(8,128)(2,1)} %get-tuple-element.33), channel_id=1, source_target_pairs={{8,0},{9,1},{10,2},{11,3},{12,4},{13,5},{14,6},{15,7},{24,16},{25,... | collective-permute-start | bytes 786440 | tf_op jit(solution)/shard_map/ppermute | solution.py:355
  67.0 1.3 %collective-permute-start.7 = (bf16[256,512]{1,0:T(8,128)(2,1)}, bf16[256,512]{1,0:T(8,128)(2,1)S(1)}, u32[]{:S(2)}, u32[]{:S(2)}) collective-permute-start(bf16[256,512]{1,0:T(8,128)(2,1)} %get-tuple-element.34), channel_id=1, source_target_pairs={{6,0},{7,1},{8,2},{9,3},{10,4},{11,5},{12,6},{13,7},{14,8},{15,9},... | collective-permute-start | bytes 786440 | tf_op jit(solution)/shard_map/ppermute | solution.py:355
  68.3 1.3 %collective-permute-start.8 = (bf16[256,512]{1,0:T(8,128)(2,1)}, bf16[256,512]{1,0:T(8,128)(2,1)S(1)}, u32[]{:S(2)}, u32[]{:S(2)}) collective-permute-start(bf16[256,512]{1,0:T(8,128)(2,1)} %get-tuple-element.35), channel_id=1, source_target_pairs={{4,0},{5,1},{6,2},{7,3},{8,4},{9,5},{10,6},{11,7},{12,8},{13,9},{1... | collective-permute-start | bytes 786440 | tf_op jit(solution)/shard_map/ppermute | solution.py:355
  69.6 1.3 %collective-permute-start.9 = (bf16[256,512]{1,0:T(8,128)(2,1)}, bf16[256,512]{1,0:T(8,128)(2,1)S(1)}, u32[]{:S(2)}, u32[]{:S(2)}) collective-permute-start(bf16[256,512]{1,0:T(8,128)(2,1)} %get-tuple-element.36), channel_id=1, source_target_pairs={{2,0},{3,1},{4,2},{5,3},{6,4},{7,5},{8,6},{9,7},{10,8},{11,9},{12,... | collective-permute-start | bytes 786440 | tf_op jit(solution)/shard_map/ppermute | solution.py:355
  71.6 15.3 %all-to-all-start = ((f32[32,1,256]{2,1,0:T(1,128)}), f32[32,1,256]{2,1,0:T(1,128)S(1)}, u32[]{:S(2)}, u32[]{:S(2)}) async-start(f32[32,1,256]{2,1,0:T(1,128)} %broadcast_in_dim.79), calls=%async_computation | async-start | bytes 65536 | tf_op jit(solution)/shard_map/all_to_all | solution.py:350
  86.9 3.7 %collective-permute-start.5 = (bf16[128,2048]{1,0:T(8,128)(2,1)}, bf16[128,2048]{1,0:T(8,128)(2,1)S(1)}, u32[]{:S(2)}, u32[]{:S(2)}) collective-permute-start(bf16[128,2048]{1,0:T(8,128)(2,1)} %copy-done.10), channel_id=1, source_target_pairs={{0,1},{1,0},{2,3},{3,2},{4,5},{5,4},{6,7},{7,6},{8,9},{9,8},{10,11... | collective-permute-start | bytes 1572872 | tf_op jit(solution)/shard_map/ppermute | solution.py:352
  90.6 8.6 %all-to-all-done = f32[32,1,256]{2,1,0:T(1,128)S(1)} async-done(((f32[32,1,256]{2,1,0:T(1,128)}), f32[32,1,256]{2,1,0:T(1,128)S(1)}, u32[]{:S(2)}, u32[]{:S(2)}) %all-to-all-start) | async-done | bytes 32800 | tf_op jit(solution)/shard_map/all_to_all | solution.py:350
  99.4 4.9 %collective-permute-start.10 = (bf16[128,512]{1,0:T(8,128)(2,1)S(1)}, bf16[128,512]{1,0:T(8,128)(2,1)S(1)}, u32[]{:S(2)}, u32[]{:S(2)}) collective-permute-start(bf16[128,512]{1,0:T(8,128)(2,1)S(1)} %constant_dynamic-slice_fusion.1), channel_id=1, source_target_pairs={{0,1},{1,0},{2,3},{3,2},{4,5},{5,4},{6,7},{7,6},{8,9},{9,8},{10,11... | collective-permute-start | bytes 393224 | tf_op jit(solution)/shard_map/ppermute | solution.py:364
  104.9 11.6 %all-to-all-start.1 = ((f32[16,1,256]{2,1,0:T(1,128)}), f32[16,1,256]{2,1,0:T(1,128)S(1)}, u32[]{:S(2)}, u32[]{:S(2)}) async-start(f32[16,1,256]{2,1,0:T(1,128)} %broadcast_in_dim.81), calls=%async_computation.1 | async-start | bytes 32768 | tf_op jit(solution)/shard_map/all_to_all | solution.py:350
  116.5 7.3 %all-to-all-done.1 = f32[16,1,256]{2,1,0:T(1,128)S(1)} async-done(((f32[16,1,256]{2,1,0:T(1,128)}), f32[16,1,256]{2,1,0:T(1,128)S(1)}, u32[]{:S(2)}, u32[]{:S(2)}) %all-to-all-start.1) | async-done | bytes 16416 | tf_op jit(solution)/shard_map/all_to_all | solution.py:350
  124.4 0.7 maximum_select_fusion.2
  125.1 0.7 maximum_select_fusion.1
  125.8 1.2 maximum_select_fusion
  (66 shorter events, 3.9 us)
Async XLA Ops:
  0.6 13.8 %copy-start.1 = (bf16[128,4096]{1,0:T(8,128)(2,1)S(1)}, bf16[128,4096]{1,0:T(8,128)(2,1)}, u32[]{:S(2)}) copy-start(bf16[128,4096]{1,0:T(8,128)(2,1)} %q_own.1) | copy-start | bytes 3145732
  1.7 13.6 %copy-start = (bf16[128,4096]{1,0:T(8,128)(2,1)S(1)}, bf16[128,4096]{1,0:T(8,128)(2,1)}, u32[]{:S(2)}) copy-start(bf16[128,4096]{1,0:T(8,128)(2,1)} %g_own) | copy-start | bytes 3145732
  1.7 9.9 %collective-permute-start = (bf16[128,512]{1,0:T(8,128)(2,1)S(1)}, bf16[128,512]{1,0:T(8,128)(2,1)S(1)}, u32[]{:S(2)}, u32[]{:S(2)}) collective-permute-start(bf16[128,512]{1,0:T(8,128)(2,1)S(1)} %pad_maximum_fusion.5), channel_id=1, source_target_pairs={{0,1},{1,0},{2,3},{3,2},{4,5},{5,4},{6,7},{7,6},{8,9},{9,8},{10,11... | collective-permute-start | bytes 393224 | tf_op jit(solution)/shard_map/ppermute | solution.py:305
  11.7 9.6 %copy-start.3 = (bf16[256,512]{1,0:T(8,128)(2,1)}, bf16[256,512]{1,0:T(8,128)(2,1)S(1)}, u32[]{:S(2)}) copy-start(bf16[256,512]{1,0:T(8,128)(2,1)S(1)} %pad_maximum_fusion.3.kv0) | copy-start | bytes 786436
  11.7 9.3 %copy-start.12 = (s32[1,4]{1,0:T(1,128)S(1)}, s32[1,4]{1,0:T(1,128)}, u32[]{:S(2)}) copy-start(s32[1,4]{1,0:T(1,128)} %param.14) | copy-start | bytes 52
  11.7 9.3 %collective-permute-start.2 = (bf16[256,512]{1,0:T(8,128)(2,1)S(1)}, bf16[256,512]{1,0:T(8,128)(2,1)S(1)}, u32[]{:S(2)}, u32[]{:S(2)}) collective-permute-start(bf16[256,512]{1,0:T(8,128)(2,1)S(1)} %pad_maximum_fusion.3.kv0), channel_id=1, source_target_pairs={{0,4},{1,5},{2,6},{3,7},{4,8},{5,9},{6,10},{7,11},{8,12},{9,13},{1... | collective-permute-start | bytes 786440 | tf_op jit(solution)/shard_map/ppermute | solution.py:310
  13.1 8.5 %collective-permute-start.3 = (bf16[256,512]{1,0:T(8,128)(2,1)S(1)}, bf16[256,512]{1,0:T(8,128)(2,1)S(1)}, u32[]{:S(2)}, u32[]{:S(2)}) collective-permute-start(bf16[256,512]{1,0:T(8,128)(2,1)S(1)} %pad_maximum_fusion.3.kv0), channel_id=1, source_target_pairs={{0,2},{1,3},{2,4},{3,5},{4,6},{5,7},{6,8},{7,9},{8,10},{9,11},{10,... | collective-permute-start | bytes 786440 | tf_op jit(solution)/shard_map/ppermute | solution.py:310
  18.2 14.7 %collective-permute-start.1 = (bf16[128,4224]{1,0:T(8,128)(2,1)}, bf16[128,4224]{1,0:T(8,128)(2,1)}, u32[]{:S(2)}, u32[]{:S(2)}) collective-permute-start(bf16[128,4224]{1,0:T(8,128)(2,1)} %broadcast_dynamic-update-slice_fusion), channel_id=1, source_target_pairs={{0,1},{1,0},{2,3},{3,2},{4,5},{5,4},{6,7},{7,6},{8,9},{9,8},{10,11... | collective-permute-start | bytes 3244040 | tf_op jit(solution)/shard_map/ppermute | solution.py:320
  21.0 10.3 %copy-start.5 = (bf16[256,512]{1,0:T(8,128)(2,1)}, bf16[256,512]{1,0:T(8,128)(2,1)S(1)}, u32[]{:S(2)}) copy-start(bf16[256,512]{1,0:T(8,128)(2,1)S(1)} %collective-permute-done.2.kv2) | copy-start | bytes 786436
  21.6 9.7 %copy-start.7 = (bf16[256,512]{1,0:T(8,128)(2,1)}, bf16[256,512]{1,0:T(8,128)(2,1)S(1)}, u32[]{:S(2)}) copy-start(bf16[256,512]{1,0:T(8,128)(2,1)S(1)} %collective-permute-done.3.kv1) | copy-start | bytes 786436
  22.5 16.9 %collective-permute-start.4 = (bf16[512,512]{1,0:T(8,128)(2,1)}, bf16[512,512]{1,0:T(8,128)(2,1)}, u32[]{:S(2)}, u32[]{:S(2)}) collective-permute-start(bf16[512,512]{1,0:T(8,128)(2,1)} %pad_maximum_fusion.2), channel_id=1, source_target_pairs={{0,4},{1,5},{2,6},{3,7},{4,8},{5,9},{6,10},{7,11},{8,12},{9,13},{1... | collective-permute-start | bytes 1572872 | tf_op jit(solution)/shard_map/ppermute | solution.py:310
  31.5 2.2 %copy-start.13 = (s32[128]{0:T(128)S(1)}, s32[128]{0:T(128)}, u32[]{:S(2)}) copy-start(s32[128]{0:T(128)} %param.15) | copy-start | bytes 1540
  31.6 2.4 %copy-start.9 = (f32[128]{0:T(128)S(1)}, f32[128]{0:T(128)}, u32[]{:S(2)}) copy-start(f32[128]{0:T(128)} %param.11) | copy-start | bytes 1540
  34.0 5.4 %copy-start.2 = (bf16[1280,128]{1,0:T(8,128)(2,1)S(1)}, bf16[1280,128]{1,0:T(8,128)(2,1)}, u32[]{:S(2)}) copy-start(bf16[1280,128]{1,0:T(8,128)(2,1)} %select_convert_fusion.kaug) | copy-start | bytes 983044
  34.0 5.4 %copy-start.4 = (bf16[256,512]{1,0:T(8,128)(2,1)S(1)}, bf16[256,512]{1,0:T(8,128)(2,1)}, u32[]{:S(2)}) copy-start(bf16[256,512]{1,0:T(8,128)(2,1)} %copy-done.3) | copy-start | bytes 786436
  34.0 5.4 %copy-start.6 = (bf16[256,512]{1,0:T(8,128)(2,1)S(1)}, bf16[256,512]{1,0:T(8,128)(2,1)}, u32[]{:S(2)}) copy-start(bf16[256,512]{1,0:T(8,128)(2,1)} %copy-done.5) | copy-start | bytes 786436
  34.0 5.4 %copy-start.8 = (bf16[256,512]{1,0:T(8,128)(2,1)S(1)}, bf16[256,512]{1,0:T(8,128)(2,1)}, u32[]{:S(2)}) copy-start(bf16[256,512]{1,0:T(8,128)(2,1)} %copy-done.7) | copy-start | bytes 786436
  34.0 5.4 %copy-start.11 = (f32[128]{0:T(128)S(1)}, f32[128]{0:T(128)}, u32[]{:S(2)}) copy-start(f32[128]{0:T(128)} %param.12) | copy-start | bytes 1540
  64.9 0.8 copy-start.10
  65.7 33.5 %collective-permute-start.6 = (bf16[256,512]{1,0:T(8,128)(2,1)}, bf16[256,512]{1,0:T(8,128)(2,1)S(1)}, u32[]{:S(2)}, u32[]{:S(2)}) collective-permute-start(bf16[256,512]{1,0:T(8,128)(2,1)} %get-tuple-element.33), channel_id=1, source_target_pairs={{8,0},{9,1},{10,2},{11,3},{12,4},{13,5},{14,6},{15,7},{24,16},{25,... | collective-permute-start | bytes 786440 | tf_op jit(solution)/shard_map/ppermute | solution.py:355
  67.0 32.2 %collective-permute-start.7 = (bf16[256,512]{1,0:T(8,128)(2,1)}, bf16[256,512]{1,0:T(8,128)(2,1)S(1)}, u32[]{:S(2)}, u32[]{:S(2)}) collective-permute-start(bf16[256,512]{1,0:T(8,128)(2,1)} %get-tuple-element.34), channel_id=1, source_target_pairs={{6,0},{7,1},{8,2},{9,3},{10,4},{11,5},{12,6},{13,7},{14,8},{15,9},... | collective-permute-start | bytes 786440 | tf_op jit(solution)/shard_map/ppermute | solution.py:355
  68.3 30.9 %collective-permute-start.8 = (bf16[256,512]{1,0:T(8,128)(2,1)}, bf16[256,512]{1,0:T(8,128)(2,1)S(1)}, u32[]{:S(2)}, u32[]{:S(2)}) collective-permute-start(bf16[256,512]{1,0:T(8,128)(2,1)} %get-tuple-element.35), channel_id=1, source_target_pairs={{4,0},{5,1},{6,2},{7,3},{8,4},{9,5},{10,6},{11,7},{12,8},{13,9},{1... | collective-permute-start | bytes 786440 | tf_op jit(solution)/shard_map/ppermute | solution.py:355
  69.6 29.6 %collective-permute-start.9 = (bf16[256,512]{1,0:T(8,128)(2,1)}, bf16[256,512]{1,0:T(8,128)(2,1)S(1)}, u32[]{:S(2)}, u32[]{:S(2)}) collective-permute-start(bf16[256,512]{1,0:T(8,128)(2,1)} %get-tuple-element.36), channel_id=1, source_target_pairs={{2,0},{3,1},{4,2},{5,3},{6,4},{7,5},{8,6},{9,7},{10,8},{11,9},{12,... | collective-permute-start | bytes 786440 | tf_op jit(solution)/shard_map/ppermute | solution.py:355
  71.6 27.6 %all-to-all-start = ((f32[32,1,256]{2,1,0:T(1,128)}), f32[32,1,256]{2,1,0:T(1,128)S(1)}, u32[]{:S(2)}, u32[]{:S(2)}) async-start(f32[32,1,256]{2,1,0:T(1,128)} %broadcast_in_dim.79), calls=%async_computation | async-start | bytes 65536 | tf_op jit(solution)/shard_map/all_to_all | solution.py:350
  86.9 38.9 %collective-permute-start.5 = (bf16[128,2048]{1,0:T(8,128)(2,1)}, bf16[128,2048]{1,0:T(8,128)(2,1)S(1)}, u32[]{:S(2)}, u32[]{:S(2)}) collective-permute-start(bf16[128,2048]{1,0:T(8,128)(2,1)} %copy-done.10), channel_id=1, source_target_pairs={{0,1},{1,0},{2,3},{3,2},{4,5},{5,4},{6,7},{7,6},{8,9},{9,8},{10,11... | collective-permute-start | bytes 1572872 | tf_op jit(solution)/shard_map/ppermute | solution.py:352
  99.4 25.0 %collective-permute-start.10 = (bf16[128,512]{1,0:T(8,128)(2,1)S(1)}, bf16[128,512]{1,0:T(8,128)(2,1)S(1)}, u32[]{:S(2)}, u32[]{:S(2)}) collective-permute-start(bf16[128,512]{1,0:T(8,128)(2,1)S(1)} %constant_dynamic-slice_fusion.1), channel_id=1, source_target_pairs={{0,1},{1,0},{2,3},{3,2},{4,5},{5,4},{6,7},{7,6},{8,9},{9,8},{10,11... | collective-permute-start | bytes 393224 | tf_op jit(solution)/shard_map/ppermute | solution.py:364
  104.9 18.9 %all-to-all-start.1 = ((f32[16,1,256]{2,1,0:T(1,128)}), f32[16,1,256]{2,1,0:T(1,128)S(1)}, u32[]{:S(2)}, u32[]{:S(2)}) async-start(f32[16,1,256]{2,1,0:T(1,128)} %broadcast_in_dim.81), calls=%async_computation.1 | async-start | bytes 32768 | tf_op jit(solution)/shard_map/all_to_all | solution.py:350

commit v4 on v3

--- a/solution.py
+++ b/solution.py
@@ -355,11 +355,10 @@
         return lax.ppermute(x, "tensor", [(t + 2 * n, t) for t in range(size - 2 * n)])
 
     back = [earlier(part, n) for n, part in zip(range(BACK, 0, -1), parts)]
-    gains, back = lax.optimization_barrier((gathered_sum(gains, "dp"), back))
-    gains = gathered_sum(gains, "tensor")
     for part in back:
         dkv = dkv + part.astype(f32)
-    dkv = dkv.astype(bf16)
+    gains, dkv = lax.optimization_barrier((gathered_sum(gains, "dp"), dkv.astype(bf16)))
+    gains = gathered_sum(gains, "tensor")
     dkv_mine = lax.dynamic_slice_in_dim(dkv, core * ROWS, ROWS, 0)
     dkv_far = lax.ppermute(lax.dynamic_slice_in_dim(dkv, (1 - core) * ROWS, ROWS, 0), "tensor", swap)
 

time: 128 us -> 128 us (level)
  no operation moved by 1% of the time
where the time goes in v4:
time: 128 us; the launch traced here: 127 us
  starting transfers between devices  61.4 us (48%)
  Pallas kernels  30.8 us (24%)
  waiting for transfers between devices  16.1 us (13%)
  other arithmetic  10.5 us (8%)
  local copies, waits for them, and re-layouts  7 us (5%)
    all_to_all x2, starting transfers between devices, gathered_sum(): return jnp.sum(lax.all_to_all(spread, axis, 0, 0, tiled=True), axis=0)  26.9 us
    pallas_call x1, Pallas kernels, attend(): pl.pallas_call(attend_kernel, grid_spec=pltpu.PrefetchScalarGridSpec(num_...  25.4 us
    all_to_all x2, waiting for transfers between devices, gathered_sum(): return jnp.sum(lax.all_to_all(spread, axis, 0, 0, tiled=True), axis=0)  15.8 us
    ppermute x3, starting transfers between devices, later(): lax.ppermute(x, 'tensor', [(t, t + 2 * n) for t in range(size - 2 * n)])  9.15 us
    ppermute x1, starting transfers between devices, local(): kv_other = lax.ppermute(half(1 - core), 'tensor', swap)  8.92 us
    pallas_call x1, Pallas kernels, queries(): pl.pallas_call(query_kernel, grid_spec=pltpu.PrefetchScalarGridSpec(num_s...  5.37 us
    ppermute x4, starting transfers between devices, earlier(): lax.ppermute(x, 'tensor', [(t + 2 * n, t) for t in range(size - 2 * n)])  5.16 us
    ppermute x1, starting transfers between devices, local(): lax.ppermute(lax.dynamic_slice_in_dim(dkv, (1 - core) * ROWS, ROWS, 0), '...  4.85 us
  transfers between devices with their start and end apart: 13, of which 3 were waited for; matrix products, arithmetic and copies ran while one was open for 11% of the time, Pallas kernels for 4%

profile of v4, /device:TPU:1, one launch (start us, length us, event | category | flops | bytes accessed | tf_op | source)
XLA Modules:
  0.0 127.0 jit_solution(14060301574632340640)
XLA Ops:
  0.7 1.0 constant_dynamic-slice_fusion.8
  1.7 8.9 %collective-permute-start = (bf16[128,512]{1,0:T(8,128)(2,1)S(1)}, bf16[128,512]{1,0:T(8,128)(2,1)S(1)}, u32[]{:S(2)}, u32[]{:S(2)}) collective-permute-start(bf16[128,512]{1,0:T(8,128)(2,1)S(1)} %pad_maximum_fusion.5), channel_id=1, source_target_pairs={{0,1},{1,0},{2,3},{3,2},{4,5},{5,4},{6,7},{7,6},{8,9},{9,8},{10,11... | collective-permute-start | bytes 393224 | tf_op jit(solution)/shard_map/ppermute | solution.py:305
  10.7 0.7 convert_element_type.47
  11.7 1.4 %collective-permute-start.2 = (bf16[256,512]{1,0:T(8,128)(2,1)S(1)}, bf16[256,512]{1,0:T(8,128)(2,1)S(1)}, u32[]{:S(2)}, u32[]{:S(2)}) collective-permute-start(bf16[256,512]{1,0:T(8,128)(2,1)S(1)} %pad_maximum_fusion.3.kv0), channel_id=1, source_target_pairs={{0,4},{1,5},{2,6},{3,7},{4,8},{5,9},{6,10},{7,11},{8,12},{9,13},{1... | collective-permute-start | bytes 786440 | tf_op jit(solution)/shard_map/ppermute | solution.py:310
  13.1 1.3 %collective-permute-start.3 = (bf16[256,512]{1,0:T(8,128)(2,1)S(1)}, bf16[256,512]{1,0:T(8,128)(2,1)S(1)}, u32[]{:S(2)}, u32[]{:S(2)}) collective-permute-start(bf16[256,512]{1,0:T(8,128)(2,1)S(1)} %pad_maximum_fusion.3.kv0), channel_id=1, source_target_pairs={{0,2},{1,3},{2,4},{3,5},{4,6},{5,7},{6,8},{7,9},{8,10},{9,11},{10,... | collective-permute-start | bytes 786440 | tf_op jit(solution)/shard_map/ppermute | solution.py:310
  14.5 0.8 dynamic-slice_dynamic-update-slice_fusion.3
  15.2 0.8 dynamic-slice_dynamic-update-slice_fusion.2
  16.0 0.8 dynamic-slice_dynamic-update-slice_fusion.1
  16.8 0.7 dynamic-slice_dynamic-update-slice_fusion
  17.5 0.7 broadcast_dynamic-update-slice_fusion
  18.2 2.8 %collective-permute-start.1 = (bf16[128,4224]{1,0:T(8,128)(2,1)}, bf16[128,4224]{1,0:T(8,128)(2,1)}, u32[]{:S(2)}, u32[]{:S(2)}) collective-permute-start(bf16[128,4224]{1,0:T(8,128)(2,1)} %broadcast_dynamic-update-slice_fusion), channel_id=1, source_target_pairs={{0,1},{1,0},{2,3},{3,2},{4,5},{5,4},{6,7},{7,6},{8,9},{9,8},{10,11... | collective-permute-start | bytes 3244040 | tf_op jit(solution)/shard_map/ppermute | solution.py:320
  21.6 0.9 pad_maximum_fusion.2
  22.5 6.4 %collective-permute-start.4 = (bf16[512,512]{1,0:T(8,128)(2,1)}, bf16[512,512]{1,0:T(8,128)(2,1)}, u32[]{:S(2)}, u32[]{:S(2)}) collective-permute-start(bf16[512,512]{1,0:T(8,128)(2,1)} %pad_maximum_fusion.2), channel_id=1, source_target_pairs={{0,4},{1,5},{2,6},{3,7},{4,8},{5,9},{6,10},{7,11},{8,12},{9,13},{1... | collective-permute-start | bytes 1572872 | tf_op jit(solution)/shard_map/ppermute | solution.py:310
  28.9 2.4 %fusion = (f32[1280,64]{1,0:T(8,128)S(1)}, f32[1280,64]{1,0:T(8,128)S(1)}, f32[1280,64]{1,0:T(8,128)S(1)}) fusion(f32[64]{0:T(128)S(1)} %multiply_power_fusion, f32[1280]{0:T(1024)S(1)} %subtract_convert_fusion), kind=kLoop, calls=%fused_computation.14 | loop fusion | flops 163840 | bytes 988416 | tf_op jit(solution)/shard_map/neg | solution.py:328
  31.8 1.0 select_convert_fusion.kaug
  32.9 0.9 multiply_reduce_fusion
  34.0 5.4 %queries.1 = (bf16[2,2,1024,256]{3,2,1,0:T(8,128)(2,1)S(1)}, bf16[2,2,1024,128]{3,2,1,0:T(8,128)(2,1)S(1)}) custom-call(s32[1]{0:T(128)} %bitcast.core_ref, bf16[128,4096]{1,0:T(8,128)(2,1)S(1)} %copy-done.1, bf16[128,4096]{1,0:T(8,128)(2,1)S(1)} %copy-done, bf16[128,4224]{1,0:T(8,128)(2,1)} %collective-permute-done.1.rq.q_far, ...), custom_call_target="tpu_custom_call" | custom-call | flops 20971520 | bytes 5242880 | tf_op jit(solution)/shard_map/queries/pallas_call | solution.py:209
  39.5 25.4 %attend_back.1 = (bf16[128,2048]{1,0:T(8,128)(2,1)S(1)}, bf16[128,2048]{1,0:T(8,128)(2,1)S(1)}, bf16[256,512]{1,0:T(8,128)(2,1)}, bf16[256,512]{1,0:T(8,128)(2,1...) custom-call(s32[1]{0:T(128)} %bitcast.core_ref, ...), custom_call_target="tpu_custom_call" | custom-call | flops 6039797760 | bytes 4194304 | tf_op jit(solution)/shard_map/attend_back/pallas_call | solution.py:239
  64.9 0.8 copy-done.10
  65.7 1.3 %collective-permute-start.6 = (bf16[256,512]{1,0:T(8,128)(2,1)}, bf16[256,512]{1,0:T(8,128)(2,1)S(1)}, u32[]{:S(2)}, u32[]{:S(2)}) collective-permute-start(bf16[256,512]{1,0:T(8,128)(2,1)} %get-tuple-element.30), channel_id=1, source_target_pairs={{8,0},{9,1},{10,2},{11,3},{12,4},{13,5},{14,6},{15,7},{24,16},{25,... | collective-permute-start | bytes 786440 | tf_op jit(solution)/shard_map/ppermute | solution.py:355
  67.0 1.3 %collective-permute-start.7 = (bf16[256,512]{1,0:T(8,128)(2,1)}, bf16[256,512]{1,0:T(8,128)(2,1)S(1)}, u32[]{:S(2)}, u32[]{:S(2)}) collective-permute-start(bf16[256,512]{1,0:T(8,128)(2,1)} %get-tuple-element.31), channel_id=1, source_target_pairs={{6,0},{7,1},{8,2},{9,3},{10,4},{11,5},{12,6},{13,7},{14,8},{15,9},... | collective-permute-start | bytes 786440 | tf_op jit(solution)/shard_map/ppermute | solution.py:355
  68.3 1.3 %collective-permute-start.8 = (bf16[256,512]{1,0:T(8,128)(2,1)}, bf16[256,512]{1,0:T(8,128)(2,1)S(1)}, u32[]{:S(2)}, u32[]{:S(2)}) collective-permute-start(bf16[256,512]{1,0:T(8,128)(2,1)} %get-tuple-element.32), channel_id=1, source_target_pairs={{4,0},{5,1},{6,2},{7,3},{8,4},{9,5},{10,6},{11,7},{12,8},{13,9},{1... | collective-permute-start | bytes 786440 | tf_op jit(solution)/shard_map/ppermute | solution.py:355
  69.6 1.3 %collective-permute-start.9 = (bf16[256,512]{1,0:T(8,128)(2,1)}, bf16[256,512]{1,0:T(8,128)(2,1)S(1)}, u32[]{:S(2)}, u32[]{:S(2)}) collective-permute-start(bf16[256,512]{1,0:T(8,128)(2,1)} %get-tuple-element.33), channel_id=1, source_target_pairs={{2,0},{3,1},{4,2},{5,3},{6,4},{7,5},{8,6},{9,7},{10,8},{11,9},{12,... | collective-permute-start | bytes 786440 | tf_op jit(solution)/shard_map/ppermute | solution.py:355
  71.6 15.3 %all-to-all-start = ((f32[32,1,256]{2,1,0:T(1,128)}), f32[32,1,256]{2,1,0:T(1,128)S(1)}, u32[]{:S(2)}, u32[]{:S(2)}) async-start(f32[32,1,256]{2,1,0:T(1,128)} %broadcast_in_dim.79), calls=%async_computation | async-start | bytes 65536 | tf_op jit(solution)/shard_map/all_to_all | solution.py:350
  86.9 3.7 %collective-permute-start.5 = (bf16[128,2048]{1,0:T(8,128)(2,1)}, bf16[128,2048]{1,0:T(8,128)(2,1)S(1)}, u32[]{:S(2)}, u32[]{:S(2)}) collective-permute-start(bf16[128,2048]{1,0:T(8,128)(2,1)} %copy-done.10), channel_id=1, source_target_pairs={{0,1},{1,0},{2,3},{3,2},{4,5},{5,4},{6,7},{7,6},{8,9},{9,8},{10,11... | collective-permute-start | bytes 1572872 | tf_op jit(solution)/shard_map/ppermute | solution.py:352
  90.6 8.6 %all-to-all-done = f32[32,1,256]{2,1,0:T(1,128)S(1)} async-done(((f32[32,1,256]{2,1,0:T(1,128)}), f32[32,1,256]{2,1,0:T(1,128)S(1)}, u32[]{:S(2)}, u32[]{:S(2)}) %all-to-all-start) | async-done | bytes 32800 | tf_op jit(solution)/shard_map/all_to_all | solution.py:350
  99.4 4.9 %collective-permute-start.10 = (bf16[128,512]{1,0:T(8,128)(2,1)S(1)}, bf16[128,512]{1,0:T(8,128)(2,1)S(1)}, u32[]{:S(2)}, u32[]{:S(2)}) collective-permute-start(bf16[128,512]{1,0:T(8,128)(2,1)S(1)} %constant_dynamic-slice_fusion.1), channel_id=1, source_target_pairs={{0,1},{1,0},{2,3},{3,2},{4,5},{5,4},{6,7},{7,6},{8,9},{9,8},{10,11... | collective-permute-start | bytes 393224 | tf_op jit(solution)/shard_map/ppermute | solution.py:363
  104.9 11.6 %all-to-all-start.1 = ((f32[16,1,256]{2,1,0:T(1,128)}), f32[16,1,256]{2,1,0:T(1,128)S(1)}, u32[]{:S(2)}, u32[]{:S(2)}) async-start(f32[16,1,256]{2,1,0:T(1,128)} %broadcast_in_dim.81), calls=%async_computation.1 | async-start | bytes 32768 | tf_op jit(solution)/shard_map/all_to_all | solution.py:350
  116.5 7.3 %all-to-all-done.1 = f32[16,1,256]{2,1,0:T(1,128)S(1)} async-done(((f32[16,1,256]{2,1,0:T(1,128)}), f32[16,1,256]{2,1,0:T(1,128)S(1)}, u32[]{:S(2)}, u32[]{:S(2)}) %all-to-all-start.1) | async-done | bytes 16416 | tf_op jit(solution)/shard_map/all_to_all | solution.py:350
  124.4 0.7 maximum_select_fusion.2
  125.1 0.7 maximum_select_fusion.1
  125.8 1.2 maximum_select_fusion
  (66 shorter events, 3.9 us)
Async XLA Ops:
  0.6 13.8 %copy-start.1 = (bf16[128,4096]{1,0:T(8,128)(2,1)S(1)}, bf16[128,4096]{1,0:T(8,128)(2,1)}, u32[]{:S(2)}) copy-start(bf16[128,4096]{1,0:T(8,128)(2,1)} %q_own.1) | copy-start | bytes 3145732
  1.7 13.6 %copy-start = (bf16[128,4096]{1,0:T(8,128)(2,1)S(1)}, bf16[128,4096]{1,0:T(8,128)(2,1)}, u32[]{:S(2)}) copy-start(bf16[128,4096]{1,0:T(8,128)(2,1)} %g_own) | copy-start | bytes 3145732
  1.7 9.9 %collective-permute-start = (bf16[128,512]{1,0:T(8,128)(2,1)S(1)}, bf16[128,512]{1,0:T(8,128)(2,1)S(1)}, u32[]{:S(2)}, u32[]{:S(2)}) collective-permute-start(bf16[128,512]{1,0:T(8,128)(2,1)S(1)} %pad_maximum_fusion.5), channel_id=1, source_target_pairs={{0,1},{1,0},{2,3},{3,2},{4,5},{5,4},{6,7},{7,6},{8,9},{9,8},{10,11... | collective-permute-start | bytes 393224 | tf_op jit(solution)/shard_map/ppermute | solution.py:305
  11.7 9.6 %copy-start.3 = (bf16[256,512]{1,0:T(8,128)(2,1)}, bf16[256,512]{1,0:T(8,128)(2,1)S(1)}, u32[]{:S(2)}) copy-start(bf16[256,512]{1,0:T(8,128)(2,1)S(1)} %pad_maximum_fusion.3.kv0) | copy-start | bytes 786436
  11.7 9.3 %copy-start.12 = (s32[1,4]{1,0:T(1,128)S(1)}, s32[1,4]{1,0:T(1,128)}, u32[]{:S(2)}) copy-start(s32[1,4]{1,0:T(1,128)} %param.14) | copy-start | bytes 52
  11.7 9.3 %collective-permute-start.2 = (bf16[256,512]{1,0:T(8,128)(2,1)S(1)}, bf16[256,512]{1,0:T(8,128)(2,1)S(1)}, u32[]{:S(2)}, u32[]{:S(2)}) collective-permute-start(bf16[256,512]{1,0:T(8,128)(2,1)S(1)} %pad_maximum_fusion.3.kv0), channel_id=1, source_target_pairs={{0,4},{1,5},{2,6},{3,7},{4,8},{5,9},{6,10},{7,11},{8,12},{9,13},{1... | collective-permute-start | bytes 786440 | tf_op jit(solution)/shard_map/ppermute | solution.py:310
  13.1 8.5 %collective-permute-start.3 = (bf16[256,512]{1,0:T(8,128)(2,1)S(1)}, bf16[256,512]{1,0:T(8,128)(2,1)S(1)}, u32[]{:S(2)}, u32[]{:S(2)}) collective-permute-start(bf16[256,512]{1,0:T(8,128)(2,1)S(1)} %pad_maximum_fusion.3.kv0), channel_id=1, source_target_pairs={{0,2},{1,3},{2,4},{3,5},{4,6},{5,7},{6,8},{7,9},{8,10},{9,11},{10,... | collective-permute-start | bytes 786440 | tf_op jit(solution)/shard_map/ppermute | solution.py:310
  18.2 14.7 %collective-permute-start.1 = (bf16[128,4224]{1,0:T(8,128)(2,1)}, bf16[128,4224]{1,0:T(8,128)(2,1)}, u32[]{:S(2)}, u32[]{:S(2)}) collective-permute-start(bf16[128,4224]{1,0:T(8,128)(2,1)} %broadcast_dynamic-update-slice_fusion), channel_id=1, source_target_pairs={{0,1},{1,0},{2,3},{3,2},{4,5},{5,4},{6,7},{7,6},{8,9},{9,8},{10,11... | collective-permute-start | bytes 3244040 | tf_op jit(solution)/shard_map/ppermute | solution.py:320
  21.0 10.3 %copy-start.5 = (bf16[256,512]{1,0:T(8,128)(2,1)}, bf16[256,512]{1,0:T(8,128)(2,1)S(1)}, u32[]{:S(2)}) copy-start(bf16[256,512]{1,0:T(8,128)(2,1)S(1)} %collective-permute-done.2.kv2) | copy-start | bytes 786436
  21.6 9.7 %copy-start.7 = (bf16[256,512]{1,0:T(8,128)(2,1)}, bf16[256,512]{1,0:T(8,128)(2,1)S(1)}, u32[]{:S(2)}) copy-start(bf16[256,512]{1,0:T(8,128)(2,1)S(1)} %collective-permute-done.3.kv1) | copy-start | bytes 786436
  22.5 16.9 %collective-permute-start.4 = (bf16[512,512]{1,0:T(8,128)(2,1)}, bf16[512,512]{1,0:T(8,128)(2,1)}, u32[]{:S(2)}, u32[]{:S(2)}) collective-permute-start(bf16[512,512]{1,0:T(8,128)(2,1)} %pad_maximum_fusion.2), channel_id=1, source_target_pairs={{0,4},{1,5},{2,6},{3,7},{4,8},{5,9},{6,10},{7,11},{8,12},{9,13},{1... | collective-permute-start | bytes 1572872 | tf_op jit(solution)/shard_map/ppermute | solution.py:310
  31.5 2.2 %copy-start.13 = (s32[128]{0:T(128)S(1)}, s32[128]{0:T(128)}, u32[]{:S(2)}) copy-start(s32[128]{0:T(128)} %param.15) | copy-start | bytes 1540
  31.6 2.4 %copy-start.9 = (f32[128]{0:T(128)S(1)}, f32[128]{0:T(128)}, u32[]{:S(2)}) copy-start(f32[128]{0:T(128)} %param.11) | copy-start | bytes 1540
  34.0 5.4 %copy-start.2 = (bf16[1280,128]{1,0:T(8,128)(2,1)S(1)}, bf16[1280,128]{1,0:T(8,128)(2,1)}, u32[]{:S(2)}) copy-start(bf16[1280,128]{1,0:T(8,128)(2,1)} %select_convert_fusion.kaug) | copy-start | bytes 983044
  34.0 5.4 %copy-start.4 = (bf16[256,512]{1,0:T(8,128)(2,1)S(1)}, bf16[256,512]{1,0:T(8,128)(2,1)}, u32[]{:S(2)}) copy-start(bf16[256,512]{1,0:T(8,128)(2,1)} %copy-done.3) | copy-start | bytes 786436
  34.0 5.4 %copy-start.6 = (bf16[256,512]{1,0:T(8,128)(2,1)S(1)}, bf16[256,512]{1,0:T(8,128)(2,1)}, u32[]{:S(2)}) copy-start(bf16[256,512]{1,0:T(8,128)(2,1)} %copy-done.5) | copy-start | bytes 786436
  34.0 5.4 %copy-start.8 = (bf16[256,512]{1,0:T(8,128)(2,1)S(1)}, bf16[256,512]{1,0:T(8,128)(2,1)}, u32[]{:S(2)}) copy-start(bf16[256,512]{1,0:T(8,128)(2,1)} %copy-done.7) | copy-start | bytes 786436
  34.0 5.4 %copy-start.11 = (f32[128]{0:T(128)S(1)}, f32[128]{0:T(128)}, u32[]{:S(2)}) copy-start(f32[128]{0:T(128)} %param.12) | copy-start | bytes 1540
  64.9 0.8 copy-start.10
  65.7 33.5 %collective-permute-start.6 = (bf16[256,512]{1,0:T(8,128)(2,1)}, bf16[256,512]{1,0:T(8,128)(2,1)S(1)}, u32[]{:S(2)}, u32[]{:S(2)}) collective-permute-start(bf16[256,512]{1,0:T(8,128)(2,1)} %get-tuple-element.30), channel_id=1, source_target_pairs={{8,0},{9,1},{10,2},{11,3},{12,4},{13,5},{14,6},{15,7},{24,16},{25,... | collective-permute-start | bytes 786440 | tf_op jit(solution)/shard_map/ppermute | solution.py:355
  67.0 32.2 %collective-permute-start.7 = (bf16[256,512]{1,0:T(8,128)(2,1)}, bf16[256,512]{1,0:T(8,128)(2,1)S(1)}, u32[]{:S(2)}, u32[]{:S(2)}) collective-permute-start(bf16[256,512]{1,0:T(8,128)(2,1)} %get-tuple-element.31), channel_id=1, source_target_pairs={{6,0},{7,1},{8,2},{9,3},{10,4},{11,5},{12,6},{13,7},{14,8},{15,9},... | collective-permute-start | bytes 786440 | tf_op jit(solution)/shard_map/ppermute | solution.py:355
  68.3 30.9 %collective-permute-start.8 = (bf16[256,512]{1,0:T(8,128)(2,1)}, bf16[256,512]{1,0:T(8,128)(2,1)S(1)}, u32[]{:S(2)}, u32[]{:S(2)}) collective-permute-start(bf16[256,512]{1,0:T(8,128)(2,1)} %get-tuple-element.32), channel_id=1, source_target_pairs={{4,0},{5,1},{6,2},{7,3},{8,4},{9,5},{10,6},{11,7},{12,8},{13,9},{1... | collective-permute-start | bytes 786440 | tf_op jit(solution)/shard_map/ppermute | solution.py:355
  69.6 29.6 %collective-permute-start.9 = (bf16[256,512]{1,0:T(8,128)(2,1)}, bf16[256,512]{1,0:T(8,128)(2,1)S(1)}, u32[]{:S(2)}, u32[]{:S(2)}) collective-permute-start(bf16[256,512]{1,0:T(8,128)(2,1)} %get-tuple-element.33), channel_id=1, source_target_pairs={{2,0},{3,1},{4,2},{5,3},{6,4},{7,5},{8,6},{9,7},{10,8},{11,9},{12,... | collective-permute-start | bytes 786440 | tf_op jit(solution)/shard_map/ppermute | solution.py:355
  71.6 27.6 %all-to-all-start = ((f32[32,1,256]{2,1,0:T(1,128)}), f32[32,1,256]{2,1,0:T(1,128)S(1)}, u32[]{:S(2)}, u32[]{:S(2)}) async-start(f32[32,1,256]{2,1,0:T(1,128)} %broadcast_in_dim.79), calls=%async_computation | async-start | bytes 65536 | tf_op jit(solution)/shard_map/all_to_all | solution.py:350
  86.9 38.9 %collective-permute-start.5 = (bf16[128,2048]{1,0:T(8,128)(2,1)}, bf16[128,2048]{1,0:T(8,128)(2,1)S(1)}, u32[]{:S(2)}, u32[]{:S(2)}) collective-permute-start(bf16[128,2048]{1,0:T(8,128)(2,1)} %copy-done.10), channel_id=1, source_target_pairs={{0,1},{1,0},{2,3},{3,2},{4,5},{5,4},{6,7},{7,6},{8,9},{9,8},{10,11... | collective-permute-start | bytes 1572872 | tf_op jit(solution)/shard_map/ppermute | solution.py:352
  99.4 25.0 %collective-permute-start.10 = (bf16[128,512]{1,0:T(8,128)(2,1)S(1)}, bf16[128,512]{1,0:T(8,128)(2,1)S(1)}, u32[]{:S(2)}, u32[]{:S(2)}) collective-permute-start(bf16[128,512]{1,0:T(8,128)(2,1)S(1)} %constant_dynamic-slice_fusion.1), channel_id=1, source_target_pairs={{0,1},{1,0},{2,3},{3,2},{4,5},{5,4},{6,7},{7,6},{8,9},{9,8},{10,11... | collective-permute-start | bytes 393224 | tf_op jit(solution)/shard_map/ppermute | solution.py:363
  104.9 18.9 %all-to-all-start.1 = ((f32[16,1,256]{2,1,0:T(1,128)}), f32[16,1,256]{2,1,0:T(1,128)S(1)}, u32[]{:S(2)}, u32[]{:S(2)}) async-start(f32[16,1,256]{2,1,0:T(1,128)} %broadcast_in_dim.81), calls=%async_computation.1 | async-start | bytes 32768 | tf_op jit(solution)/shard_map/all_to_all | solution.py:350
